TPU v7x, 256 devices: a whole 4x4x8 slice. The times are simulated.
256 devices in a mesh: dp: 8 (over x, core), proto: 32 (over z, y).
Axes of the slice: x: 4, y: 4, z: 8, core: 2. Of those that a mesh axis runs over, the one named last changes fastest.
Arguments:
- teacher_emb: bfloat16 [4096, 256], P('dp'), may hold values from -6 to 6
- student_emb: bfloat16 [4096, 256], P('dp'), may hold values from -0.375 to 0.375
- prototypes: bfloat16 [256, 262144], P(None, ('dp', 'proto')), may hold values from -0.375 to 0.375
Outputs:
- total_loss: float32 [], replicated
- grad_student: float32 [4096, 256], P('dp')
- grad_prototypes: float32 [256, 262144], P(None, ('dp', 'proto'))
All inputs are finite; a program needn't handle non-finite values.
Results may differ from a plain program's by a relative error of at most 0.0089.
Values may be sent and summed in bfloat16 or wider, within the bound.
A program may use at most 128 MiB of HBM per device.

v0:
```python
import math

import jax
import jax.numpy as jnp
from jax import lax
from jax.sharding import PartitionSpec as P

ITERS = 3


TEACHER_TEMP = 0.04
STUDENT_TEMP = 0.1
NORM_EPS = 1e-06


def unit_along(values, axis_index):
    floats = values.astype(jnp.float32)
    inverse = lax.rsqrt(jnp.sum(floats * floats, axis=axis_index, keepdims=True) + NORM_EPS)
    return (floats * inverse, inverse)


def sink_mass(partial_sums):
    return lax.psum(partial_sums, ("dp", "proto"))


def shards(teacher_emb, student_emb, prototypes):
    teach_all, stud_all = (
        lax.all_gather(teacher_emb, "dp", axis=0, tiled=True),
        lax.all_gather(student_emb, "dp", axis=0, tiled=True),
    )
    row_count = teach_all.shape[0]
    own_rows = student_emb.shape[0]
    col_count = prototypes.shape[1]
    total_cols = col_count * lax.axis_size("dp") * lax.axis_size("proto")
    teach_hat = unit_along(teach_all, 1)[0].astype(jnp.bfloat16)
    stud_hat = unit_along(stud_all, 1)[0].astype(jnp.bfloat16)
    proto_unit, proto_inverse = unit_along(prototypes, 0)
    proto_hat = proto_unit.astype(jnp.bfloat16)
    expo = jnp.exp(jnp.dot(teach_hat, proto_hat, preferred_element_type=jnp.float32) / TEACHER_TEMP)
    logits = jnp.dot(stud_hat, proto_hat, preferred_element_type=jnp.float32) / STUDENT_TEMP
    stud_partial = jnp.sum(jnp.exp(logits), axis=1)
    stud_total = lax.psum(stud_partial, ("dp", "proto"))
    row_scale = jnp.ones((row_count,), jnp.float32)
    col_scale = jnp.ones((col_count,), jnp.float32)
    for step_index in range(ITERS):
        col_scale = 1.0 / (total_cols * jnp.sum(row_scale[:, None] * expo, axis=0))
        partial_rows = jnp.sum(expo * col_scale[None, :], axis=1)
        row_total = sink_mass(partial_rows)
        row_scale = 1.0 / (row_count * row_total)
    lse = jnp.log(stud_total)
    targets = row_count * row_scale[:, None] * expo * col_scale[None, :]
    probs = jnp.exp(logits - lse[:, None])
    delta = ((probs - targets) / STUDENT_TEMP).astype(jnp.bfloat16)
    cross_part = jnp.sum(targets * logits, axis=1)
    embed_part = lax.dot_general(
        delta, proto_hat, (((1,), (1,)), ((), ())), preferred_element_type=jnp.float32
    )
    dw_hat = lax.dot_general(
        stud_hat, delta, (((0,), (0,)), ((), ())), preferred_element_type=jnp.float32
    )
    start = lax.axis_index("dp") * own_rows
    embed_all, cross_all = lax.psum((embed_part, cross_part), ("dp", "proto"))
    total_loss = jnp.mean(lse - cross_all)
    dz_hat = lax.dynamic_slice_in_dim(embed_all, start, own_rows, 0)
    stud_unit, stud_inverse = unit_along(student_emb, 1)
    grad_student = stud_inverse * (
        dz_hat - stud_unit * jnp.sum(stud_unit * dz_hat, axis=1, keepdims=True)
    )
    grad_prototypes = (
        total_cols
        / math.sqrt(row_count)
        * proto_inverse
        * (dw_hat - proto_unit * jnp.sum(proto_unit * dw_hat, axis=0, keepdims=True))
    )
    return (total_loss, grad_student, grad_prototypes)


def solution(mesh):
    in_specs = (P("dp", None), P("dp", None), P(None, ("dp", "proto")))
    out_specs = (P(), P("dp", None), P(None, ("dp", "proto")))
    return jax.shard_map(shards, mesh=mesh, in_specs=in_specs, out_specs=out_specs, check_vma=False)
```

profile of v0, /device:TPU:1, one launch (start us, length us, event | category | flops | bytes accessed | tf_op | source)
XLA Modules:
  0.0 697.2 jit_solution(1163010466138057181)
XLA Ops:
  7.9 0.7 all-gather.3.cloned.1.call-update
  8.7 1.2 fusion.12
  9.9 31.9 %all-gather.5.cloned.1.call-done = bf16[4096,256]{1,0:T(8,128)(2,1)} async-done(((bf16[512,256]{1,0:T(8,128)(2,1)}), bf16[4096,256]{1,0:T(8,128)(2,1)}) %all-gather.5.cloned.1.call-update) | async-done | bytes 2097168 | tf_op jit(solution)/shard_map/all_gather | solution.py:28
  41.8 2.2 fusion.2
  44.0 8.7 %fusion.28 = (f32[1024]{0:T(1024)S(1)}, f32[4096,1024]{0,1:T(8,128)}) fusion(bf16[256,1024]{1,0:T(8,128)(2,1)} %param.5, f32[1024]{0:T(1024)S(1)} %get-tuple-element.10, bf16[4096,256]{1,0:T(8,128)(2,1)} %all-gather.5.cloned.1.call-done, f32[4096]{0:T(1024)S(1)} %add_rsqrt_fusion), kind=kOutput, calls=%fused_computation.52 | convolution fusion | flops 2159803392 | bytes 19423232 | tf_op jit(solution)/shard_map/dot_general | solution.py:39
  52.8 7.5 %multiply_reduce_fusion.5 = f32[4096]{0:T(1024)S(1)} fusion(f32[4096,1024]{0,1:T(8,128)} %get-tuple-element.12, f32[1024]{0:T(1024)S(1)} %multiply_divide_fusion.4), kind=kLoop, calls=%fused_computation.7 | loop fusion | flops 8384512 | bytes 16797696 | tf_op jit(solution)/shard_map/reduce_sum | solution.py:47
  60.3 76.9 %psum.43 = f32[4096]{0:T(1024)S(1)} all-reduce(f32[4096]{0:T(1024)S(1)} %multiply_reduce_fusion.5), channel_id=1, replica_groups=mesh['dp'=8,'proto'=32] {'dp','proto'}, use_global_device_ids=true, to_apply=%region_7.0 | all-reduce | flops 4096 | bytes 32768 | tf_op jit(solution)/shard_map/psum | solution.py:23
  137.2 7.1 %multiply_reduce_fusion.4 = f32[1024]{0:T(1024)S(1)} fusion(f32[4096,1024]{0,1:T(8,128)} %get-tuple-element.12, f32[4096]{0:T(1024)S(1)} %multiply_divide_fusion.1), kind=kLoop, calls=%fused_computation.6 | loop fusion | flops 8387584 | bytes 16797696 | tf_op jit(solution)/shard_map/reduce_sum | solution.py:46
  144.3 7.2 %multiply_reduce_fusion.3 = f32[4096]{0:T(1024)S(1)} fusion(f32[4096,1024]{0,1:T(8,128)} %get-tuple-element.12, f32[1024]{0:T(1024)S(1)} %multiply_divide_fusion.3), kind=kLoop, calls=%fused_computation.5 | loop fusion | flops 8384512 | bytes 16797696 | tf_op jit(solution)/shard_map/reduce_sum | solution.py:47
  151.4 74.2 %psum.44 = f32[4096]{0:T(1024)S(1)} all-reduce(f32[4096]{0:T(1024)S(1)} %multiply_reduce_fusion.3), channel_id=1, replica_groups=mesh['dp'=8,'proto'=32] {'dp','proto'}, use_global_device_ids=true, to_apply=%region_10.0 | all-reduce | flops 4096 | bytes 32768 | tf_op jit(solution)/shard_map/psum | solution.py:23
  225.6 7.0 %multiply_reduce_fusion.2 = f32[1024]{0:T(1024)S(1)} fusion(f32[4096,1024]{0,1:T(8,128)} %get-tuple-element.12, f32[4096]{0:T(1024)S(1)} %multiply_divide_fusion), kind=kLoop, calls=%fused_computation.4 | loop fusion | flops 8387584 | bytes 16797696 | tf_op jit(solution)/shard_map/reduce_sum | solution.py:46
  232.7 7.2 %multiply_reduce_fusion.1 = f32[4096]{0:T(1024)S(1)} fusion(f32[4096,1024]{0,1:T(8,128)} %get-tuple-element.12, f32[1024]{0:T(1024)S(1)} %multiply_divide_fusion.2), kind=kLoop, calls=%fused_computation.3 | loop fusion | flops 8384512 | bytes 16797696 | tf_op jit(solution)/shard_map/reduce_sum | solution.py:47
  239.8 73.1 %psum.45 = f32[4096]{0:T(1024)S(1)} all-reduce(f32[4096]{0:T(1024)S(1)} %multiply_reduce_fusion.1), channel_id=1, replica_groups=mesh['dp'=8,'proto'=32] {'dp','proto'}, use_global_device_ids=true, to_apply=%region_13.0 | all-reduce | flops 4096 | bytes 32768 | tf_op jit(solution)/shard_map/psum | solution.py:23
  312.9 2.2 fusion
  315.2 12.6 %exponential_reduce_fusion = (f32[4096]{0:T(1024)S(1)}, f32[4096]{0:T(1024)S(1)}, f32[4096,1024]{0,1:T(8,128)}) fusion(f32[1024]{0:T(1024)S(1)} %multiply_divide_fusion.2, f32[4096,1024]{0,1:T(8,128)} %get-tuple-element.12, f32[4096]{0:T(1024)S(1)} %divide_multiply_fusion, bf16[256,1024]{1,0:T(8,128)(2,1)S(1)} %copy-done.1, f32[1024]{0:T(1024)S(1)} %get-tuple-element.10, ...), kind=kOutput, calls=%fused_computation.9 | convolution fusion | flops 2176573440 | bytes 36249600 | tf_op jit(solution)/shard_map/dot_general | solution.py:40
  327.8 74.4 %all-reduce = (f32[4096]{0:T(1024)S(1)}, f32[4096]{0:T(1024)S(1)}) all-reduce(f32[4096]{0:T(1024)S(1)} %get-tuple-element.4, f32[4096]{0:T(1024)S(1)} %get-tuple-element.3), channel_id=1, replica_groups=mesh['dp'=8,'proto'=32] {'dp','proto'}, use_global_device_ids=true, to_apply=%region_15.0 | all-reduce | flops 8192 | bytes 65536 | tf_op jit(solution)/shard_map/psum | solution.py:62
  402.8 12.1 %multiply_convert_fusion = bf16[4096,1024]{0,1:T(8,128)(2,1)S(1)} fusion(f32[4096,1024]{0,1:T(8,128)} %get-tuple-element.12, f32[4096,1024]{0,1:T(8,128)} %get-tuple-element.13, f32[4096]{0:T(1024)S(1)} %get-tuple-element.7, f32[4096]{0:T(1024)S(1)} %divide_multiply_fusion, f32[1024]{0:T(1024)S(1)} %multiply_divide_fusion.2), kind=kLoop, calls=%fused_computation | loop fusion | flops 29360128 | bytes 41979904 | tf_op jit(solution)/shard_map/convert_element_type | solution.py:53
  414.9 3.2 copy-done.2
  418.1 4.6 fusion.23
  423.6 6.4 fusion.9
  430.0 1.2 fusion.11
  431.2 255.0 %all-reduce.3.cloned.1.call-done = f32[4096,256]{1,0:T(8,128)} async-done(((f32[4096,256]{1,0:T(8,128)}), f32[4096,256]{1,0:T(8,128)}) %all-reduce.3.cloned.1.call-update) | async-done | bytes 4194320 | tf_op jit(solution)/shard_map/psum | solution.py:62
  686.2 1.3 fusion.19
  687.5 2.0 fusion.21
  (25 shorter events, 1.7 us)
Async XLA Ops:
  7.2 34.6 %all-gather.5.cloned.1.call-start = ((), (), s32[]{:S(2)}) async-start(), calls=%async_computation.1 | async-start | bytes 2359296 | tf_op jit(solution)/shard_map/all_gather | solution.py:28
  7.9 305.0 %all-gather.3.cloned.1.call-start = ((), (), s32[]{:S(2)}) async-start(), calls=%async_computation | async-start | bytes 2359296 | tf_op jit(solution)/shard_map/all_gather | solution.py:29
  8.6 677.6 %all-reduce.3.cloned.1.call-start = ((), (), s32[]{:S(2)}) async-start(), calls=%async_computation.2 | async-start | bytes 8388608 | tf_op jit(solution)/shard_map/psum | solution.py:62
  225.6 89.6 %copy-start.1 = (bf16[256,1024]{1,0:T(8,128)(2,1)S(1)}, bf16[256,1024]{1,0:T(8,128)(2,1)}, u32[]{:S(2)}) copy-start(bf16[256,1024]{1,0:T(8,128)(2,1)} %param.5) | copy-start | bytes 1572868
  414.9 3.2 copy-start.2
  418.1 4.6 copy-start.3
  418.1 5.4 copy-start
Sparse Core Ops, SparseCore 0:
  9.9 31.8 all-gather.4
  43.7 28.0 all-gather.2
  422.8 263.3 all-reduce.2
where the time goes:
time: 699 us; the launch traced here: 697 us
  blocking collectives  299 us (43%)
  waiting for transfers between devices  288 us (41%)
  other arithmetic  58.9 us (8%)
  matrix products  32.3 us (5%)
  between operations  15.7 us (2%)
    psum x1, waiting for transfers between devices, shards(): embed_all, cross_all = lax.psum((embed_part, cross_part), ('dp', 'proto'))  255 us
    psum x3, blocking collectives, sink_mass(): return lax.psum(partial_sums, ('dp', 'proto'))  224 us
    psum x1, blocking collectives, shards(): embed_all, cross_all = lax.psum((embed_part, cross_part), ('dp', 'proto'))  74.4 us
    all_gather x1, waiting for transfers between devices, shards(): lax.all_gather(teacher_emb, 'dp', axis=0, tiled=True)  31.9 us
    reduce_sum x3, other arithmetic, shards(): partial_rows = jnp.sum(expo * col_scale[None, :], axis=1)  21.8 us
    reduce_sum x2, other arithmetic, shards(): col_scale = 1.0 / (total_cols * jnp.sum(row_scale[:, None] * expo, axis=0))  14.1 us
  transfers between devices with their start and end apart: 3, of which 2 were waited for; matrix products, arithmetic and copies ran while one was open for 8% of the time, Pallas kernels for 0%

commit v1 on v0

v1 whole, which is shorter than its diff:
```python
import functools
import math

import jax
import jax.numpy as jnp
from jax import lax
from jax.experimental import pallas as pl
from jax.experimental.pallas import tpu as pltpu
from jax.sharding import PartitionSpec as P

ITERS = 3
TEACHER_TEMP = 0.04
STUDENT_TEMP = 0.1
NORM_EPS = 1e-06
LOG2E = 1.4426950408889634
NX, NC, NY, NZ = 4, 2, 4, 8

MESH = pl.DeviceIdType.MESH
F32, BF16 = jnp.float32, jnp.bfloat16
NT = (((1,), (1,)), ((), ()))


def unit_along(values, axis):
    floats = values.astype(F32)
    inverse = lax.rsqrt(jnp.sum(floats * floats, axis=axis, keepdims=True) + NORM_EPS)
    return floats * inverse, inverse


def split_rows(vec):
    n = vec.shape[1]
    high = vec.astype(BF16).astype(F32)
    low = vec - high
    row = lax.broadcasted_iota(jnp.int32, (16, n), 0)
    both = jnp.where(row == 0, high, jnp.where(row == 1, low, 0.0))
    return both.astype(BF16)


def kernel(
    total_rows,
    total_cols,
    teach_ref,
    stud_ref,
    proto_ref,
    loss_ref,
    gs_ref,
    gp_ref,
    teach_all,
    stud_all,
    proto_all,
    protot_all,
    exp_t,
    exp_s,
    acc,
    colx,
    xy1,
    z1,
    xy2,
    z2,
    send_a,
    send_b,
    recv_a,
    recv_b,
    send_a2,
    send_b2,
    recv_a2,
    recv_b2,
    zsend,
    zrecv,
    ygather,
    dw_buf,
    dw_send,
    dw_recv,
    loss_x,
    dzt,
    ssem,
    rsem,
):
    d = lax.axis_index("dp")
    p = lax.axis_index("proto")
    x, c = d // NC, lax.rem(d, NC)
    z, y = p // NY, lax.rem(p, NY)
    own = teach_ref.shape[0]
    k_dim, cols = proto_ref.shape
    rows = NX * own
    both_cols = 2 * cols

    def at_x(k):
        return lax.rem(x + k, NX)

    def at_y(k):
        return lax.rem(y + k, NY)

    def at_z(k):
        return lax.rem(z + k, NZ)

    def dev(xx, cc, yy, zz):
        return (xx * NC + cc, zz * NY + yy)

    partner = dev(x, 1 - c, y, z)
    xy_peers = [dev(at_x(k // 4), c, at_y(k % 4), z) for k in range(1, 16)]
    z_peers = [dev(x, c, y, at_z(k)) for k in range(1, 8)]

    barrier = pltpu.get_barrier_semaphore()
    everyone = [partner] + xy_peers + z_peers
    for peer in everyone:
        pl.semaphore_signal(barrier, inc=1, device_id=peer, device_id_type=MESH)

    started = []

    def send(src, dst, peer):
        index = len(started)
        copy = pltpu.make_async_remote_copy(
            src_ref=src,
            dst_ref=dst,
            send_sem=ssem.at[index],
            recv_sem=rsem.at[index],
            device_id=peer,
            device_id_type=MESH,
        )
        copy.start()
        started.append(copy)
        return index

    def arrive(index, landed, peer):
        pltpu.make_async_remote_copy(
            src_ref=landed,
            dst_ref=landed,
            send_sem=ssem.at[index],
            recv_sem=rsem.at[index],
            device_id=peer,
            device_id_type=MESH,
        ).wait_recv()

    X_ORDER = (1, 3, 2)

    teach_hat = unit_along(teach_ref[...], 1)[0]
    teach_all[x] = jnp.transpose(teach_hat).astype(BF16)
    pl.semaphore_wait(barrier, len(everyone))
    teach_copy = {
        k: send(teach_all.at[x], teach_all.at[x], dev(at_x(k), c, y, z)) for k in X_ORDER
    }
    proto_unit, proto_inverse = unit_along(proto_ref[...], 0)
    proto_all[c] = proto_unit.astype(BF16)
    protot_all[c] = jnp.transpose(proto_unit).astype(BF16)
    protot_copy = send(protot_all.at[c], protot_all.at[c], partner)
    proto_copy = send(proto_all.at[c], proto_all.at[c], partner)
    stud_hat = unit_along(stud_ref[...], 1)[0]
    stud_all[x] = jnp.transpose(stud_hat).astype(BF16)
    stud_copy = {
        k: send(stud_all.at[x], stud_all.at[x], dev(at_x(k), c, y, z)) for k in X_ORDER
    }

    CH = 512
    half_steps = cols // CH

    def teacher_block(block, half):
        def body(i, carry):
            rows_in = pl.ds(pl.multiple_of(i * CH, CH), CH)
            rows_out = pl.ds(pl.multiple_of(half * cols + i * CH, CH), CH)
            prod = jnp.dot(
                protot_all[half, rows_in, :], teach_all[block], preferred_element_type=F32
            )
            e = jnp.exp2(prod * (LOG2E / TEACHER_TEMP))
            exp_t[block, rows_out, :] = e.astype(BF16)
            part = e[:, 0:128]
            for lane in range(128, own, 128):
                part = part + e[:, lane : lane + 128]
            acc[rows_out, :] += part
            return carry

        lax.fori_loop(0, half_steps, body, 0)

    acc[...] = jnp.zeros_like(acc)
    teacher_block(x, c)
    arrive(protot_copy, protot_all.at[1 - c], partner)
    teacher_block(x, 1 - c)
    for k in X_ORDER:
        source = at_x(NX - k)
        arrive(teach_copy[k], teach_all.at[source], dev(source, c, y, z))
        teacher_block(source, 0)
        teacher_block(source, 1)

    def column_scale(step, sums):
        colx[step, c] = sums
        index = send(colx.at[step, c], colx.at[step, c], partner)
        arrive(index, colx.at[step, 1 - c], partner)
        return 1.0 / (total_cols * (colx[step, 0] + colx[step, 1]))

    def first_column_sums():
        parts = []
        for b in range(both_cols // 128):
            t = jnp.transpose(acc[b * 128 : (b + 1) * 128, :])
            parts.append(jnp.sum(t, axis=0, keepdims=True))
        return jnp.concatenate(parts, axis=1)

    def column_sums(row_scale):
        left = split_rows(row_scale)
        total = None
        for j in range(NX):
            part = lax.dot_general(
                left[:, j * own : (j + 1) * own], exp_t[j], NT, preferred_element_type=F32
            )
            total = part if total is None else total + part
        return total[0:1] + total[1:2]

    def row_sums(col_scale):
        left = split_rows(col_scale)
        parts = []
        for j in range(NX):
            part = jnp.dot(left, exp_t[j], preferred_element_type=F32)
            parts.append(part[0:1] + part[1:2])
        return jnp.concatenate(parts, axis=1)

    xy_me = x * NY + y

    def start_xy(buf, vec):
        buf[xy_me] = vec
        return [send(buf.at[xy_me], buf.at[xy_me], peer) for peer in xy_peers]

    def finish_xy(buf, indices):
        for k, index in zip(range(1, 16), indices):
            sx, sy = at_x(NX - k // 4), at_y(NY - k % 4)
            arrive(index, buf.at[sx * NY + sy], dev(sx, c, sy, z))
        total = buf[0]
        for i in range(1, 16):
            total = total + buf[i]
        return total

    def start_z(buf, vec):
        buf[z] = vec
        return [send(buf.at[z], buf.at[z], peer) for peer in z_peers]

    def finish_z(buf, indices):
        for k, index in zip(range(1, 8), indices):
            sz = at_z(NZ - k)
            arrive(index, buf.at[sz], dev(x, c, y, sz))
        total = buf[0]
        for i in range(1, 8):
            total = total + buf[i]
        return total

    half_k, piece = k_dim // 2, k_dim // 8

    def reduce_block(which, j, value):
        low = value.astype(BF16)
        send_a[which, j] = low[:half_k]
        for q in range(NY):
            send_b[which, q, j] = low[half_k + q * piece : half_k + (q + 1) * piece]

    def start_first(which):
        a = {
            k: send(send_a.at[which, at_x(k)], recv_a.at[which, x], dev(at_x(k), c, y, z))
            for k in X_ORDER
        }
        b = {
            k: send(send_b.at[which, at_y(k)], recv_b.at[which, y], dev(x, c, at_y(k), z))
            for k in X_ORDER
        }
        return a, b

    def start_second(which, first):
        a, b = first
        recv_a[which, x] = send_a[which, x]
        recv_b[which, y] = send_b[which, y]
        for k in X_ORDER:
            source = at_x(NX - k)
            arrive(a[k], recv_a.at[which, source], dev(source, c, y, z))
        total = recv_a[which, 0].astype(F32)
        for i in range(1, NX):
            total = total + recv_a[which, i].astype(F32)
        low = total.astype(BF16)
        for q in range(NY):
            send_a2[which, q] = low[q * piece : (q + 1) * piece]
        a2 = {
            k: send(send_a2.at[which, at_y(k)], recv_a2.at[which, y], dev(x, c, at_y(k), z))
            for k in X_ORDER
        }
        for k in X_ORDER:
            source = at_y(NY - k)
            arrive(b[k], recv_b.at[which, source], dev(x, c, source, z))
        for j in range(NX):
            total = recv_b[which, 0, j].astype(F32)
            for i in range(1, NY):
                total = total + recv_b[which, i, j].astype(F32)
            send_b2[which, j] = total.astype(BF16)
        b2 = {
            k: send(send_b2.at[which, at_x(k)], recv_b2.at[which, x], dev(at_x(k), c, y, z))
            for k in X_ORDER
        }
        return a2, b2

    def finish_second(which, second):
        a2, b2 = second
        recv_a2[which, y] = send_a2[which, y]
        recv_b2[which, x] = send_b2[which, x]
        for k in X_ORDER:
            source = at_y(NY - k)
            arrive(a2[k], recv_a2.at[which, source], dev(x, c, source, z))
        for k in X_ORDER:
            source = at_x(NX - k)
            arrive(b2[k], recv_b2.at[which, source], dev(source, c, y, z))
        low = recv_a2[which, 0].astype(F32)
        high = recv_b2[which, 0].astype(F32)
        for i in range(1, 4):
            low = low + recv_a2[which, i].astype(F32)
            high = high + recv_b2[which, i].astype(F32)
        return jnp.concatenate([low, high], axis=0)

    scale = column_scale(0, first_column_sums())
    xy_copies = start_xy(xy1, row_sums(scale))

    arrive(proto_copy, proto_all.at[1 - c], partner)
    for k in X_ORDER:
        source = at_x(NX - k)
        arrive(stud_copy[k], stud_all.at[source], dev(source, c, y, z))

    def student_body(i, carry):
        block, chunk = i // (2 * half_steps), lax.rem(i, 2 * half_steps)
        half, inner = chunk // half_steps, lax.rem(chunk, half_steps)
        prod = jnp.dot(
            protot_all[half, pl.ds(pl.multiple_of(inner * CH, CH), CH), :],
            stud_all[block],
            preferred_element_type=F32,
        )
        exp_s[block, pl.ds(pl.multiple_of(chunk * CH, CH), CH), :] = jnp.exp2(
            prod * (LOG2E / STUDENT_TEMP)
        ).astype(BF16)
        return carry

    lax.fori_loop(0, NX * 2 * half_steps, student_body, 0)

    z_copies = start_z(z1, finish_xy(xy1, xy_copies))

    protos = jnp.concatenate([proto_all[0], proto_all[1]], axis=1)
    ones = jnp.ones((16, both_cols), BF16)
    stud_sums = []
    for j in range(NX):
        reduce_block(0, j, jnp.dot(protos, exp_s[j], preferred_element_type=F32))
        stud_sums.append(jnp.dot(ones, exp_s[j], preferred_element_type=F32)[0:1])
    first_p1 = start_first(0)
    row_scale = 1.0 / (total_rows * finish_z(z1, z_copies))

    scale = column_scale(1, column_sums(row_scale))
    vec = jnp.concatenate([row_sums(scale), jnp.concatenate(stud_sums, axis=1)], axis=0)
    xy_copies = start_xy(xy2.at[0], vec)
    second_p1 = start_second(0, first_p1)
    z_copies = start_z(z2.at[0], finish_xy(xy2.at[0], xy_copies))
    totals = finish_z(z2.at[0], z_copies)
    row_scale = 1.0 / (total_rows * totals[0:1])
    stud_total = totals[1:2]

    scale = column_scale(2, column_sums(row_scale))
    sums = row_sums(scale)
    scaled = (protos.astype(F32) * scale).astype(BF16)
    cross = []
    for j in range(NX):
        value = jnp.dot(scaled, exp_t[j], preferred_element_type=F32)
        reduce_block(1, j, value)
        cross.append(jnp.sum(value * stud_all[j].astype(F32), axis=0, keepdims=True))
    first_p2 = start_first(1)
    vec = jnp.concatenate([sums, jnp.concatenate(cross, axis=1)], axis=0)
    xy_copies = start_xy(xy2.at[1], vec)

    stud_factor = (1.0 / STUDENT_TEMP) / stud_total
    for h in range(2):
        total = None
        for j in range(NX):
            left = (stud_all[j].astype(F32) * stud_factor[:, j * own : (j + 1) * own]).astype(BF16)
            part = lax.dot_general(
                left, exp_s[j, h * cols : (h + 1) * cols, :], NT, preferred_element_type=F32
            )
            total = part if total is None else total + part
        dw_buf[h] = total

    z_copies = start_z(z2.at[1], finish_xy(xy2.at[1], xy_copies))
    second_p2 = start_second(1, first_p2)
    totals = finish_z(z2.at[1], z_copies)
    row_scale = 1.0 / (total_rows * totals[0:1])
    teach_factor = (total_rows / STUDENT_TEMP) * row_scale

    terms = jnp.log(stud_total) - teach_factor * totals[1:2]
    part = terms[:, 0:128]
    for lane in range(128, rows, 128):
        part = part + terms[:, lane : lane + 128]
    loss_x[c] = part
    loss_copy = send(loss_x.at[c], loss_x.at[c], partner)

    loss_x_dummy = None
    acc_rows = stud_factor[:, 0:own]
    acc_rows2 = teach_factor[:, 0:own]
    for j in range(1, NX):
        acc_rows = jnp.where(x == j, stud_factor[:, j * own : (j + 1) * own], acc_rows)
        acc_rows2 = jnp.where(x == j, teach_factor[:, j * own : (j + 1) * own], acc_rows2)
    mixed = acc_rows * finish_second(0, second_p1) - acc_rows2 * finish_second(1, second_p2)
    low = mixed.astype(BF16)
    half_own = own // 2
    for q in range(NZ):
        r = 16 * (q // 2)
        s = half_own * (q % 2)
        zsend[q] = low[r : r + 16, s : s + half_own]
    z_copies = [
        send(zsend.at[at_z(k)], zrecv.at[z], dev(x, c, y, at_z(k))) for k in range(1, NZ)
    ]

    for h in range(2):
        total = None
        for j in range(NX):
            left = (stud_all[j].astype(F32) * teach_factor[:, j * own : (j + 1) * own]).astype(BF16)
            part = lax.dot_general(
                left, exp_t[j, h * cols : (h + 1) * cols, :], NT, preferred_element_type=F32
            )
            total = part if total is None else total + part
        dw_buf[h] = dw_buf[h] - total * scale[:, h * cols : (h + 1) * cols]
    dw_send[...] = dw_buf[1 - c].astype(BF16)
    dw_copy = send(dw_send, dw_recv, partner)

    zrecv[z] = zsend[z]
    for k in range(1, NZ):
        sz = at_z(NZ - k)
        arrive(z_copies[k - 1], zrecv.at[sz], dev(x, c, y, sz))
    total = zrecv[0].astype(F32)
    for i in range(1, NZ):
        total = total + zrecv[i].astype(F32)
    ygather[y, z] = total.astype(BF16)
    z_copies = [
        send(ygather.at[y, z], ygather.at[y, z], dev(x, c, y, at_z(k))) for k in range(1, NZ)
    ]

    arrive(loss_copy, loss_x.at[1 - c], partner)
    loss_ref[...] = jnp.broadcast_to(
        jnp.sum(loss_x[0] + loss_x[1], axis=1, keepdims=True) / total_rows, loss_ref.shape
    )
    arrive(dw_copy, dw_recv, partner)
    dw_hat = dw_buf[c] + dw_recv[...].astype(F32)
    proto_unit, proto_inverse = unit_along(proto_ref[...], 0)
    gp_ref[...] = (
        (total_cols / math.sqrt(total_rows))
        * proto_inverse
        * (dw_hat - proto_unit * jnp.sum(proto_unit * dw_hat, axis=0, keepdims=True))
    )

    for k in range(1, NZ):
        sz = at_z(NZ - k)
        arrive(z_copies[k - 1], ygather.at[y, sz], dev(x, c, y, sz))
    y_copies = {
        k: send(ygather.at[y], ygather.at[y], dev(x, c, at_y(k), z)) for k in X_ORDER
    }
    for k in X_ORDER:
        source = at_y(NY - k)
        arrive(y_copies[k], ygather.at[source], dev(x, c, source, z))
    for i in range(NY):
        for q in range(NZ):
            r = 16 * (q // 2)
            s = half_own * (q % 2)
            base = i * piece + r if r < piece else half_k + i * piece + r - piece
            dzt[base : base + 16, s : s + half_own] = ygather[i, q].astype(F32)
    dz = jnp.transpose(dzt[...])
    stud_unit, stud_inverse = unit_along(stud_ref[...], 1)
    gs_ref[...] = stud_inverse * (
        dz - stud_unit * jnp.sum(stud_unit * dz, axis=1, keepdims=True)
    )
    for copy in started:
        copy.wait_send()


def solution(mesh):
    def shards(teacher_emb, student_emb, prototypes):
        own, k_dim = teacher_emb.shape
        cols = prototypes.shape[1]
        rows, both = NX * own, 2 * cols
        total_rows = own * mesh.shape["dp"]
        total_cols = cols * mesh.shape["dp"] * mesh.shape["proto"]
        vmem = pltpu.VMEM
        piece = k_dim // 8
        scratch = [
            vmem((NX, k_dim, own), BF16),
            vmem((NX, k_dim, own), BF16),
            vmem((NC, k_dim, cols), BF16),
            vmem((NC, cols, k_dim), BF16),
            vmem((NX, both, own), BF16),
            vmem((NX, both, own), BF16),
            vmem((both, 128), F32),
            vmem((ITERS, NC, 1, both), F32),
            vmem((NX * NY, 1, rows), F32),
            vmem((NZ, 1, rows), F32),
            vmem((2, NX * NY, 2, rows), F32),
            vmem((2, NZ, 2, rows), F32),
            vmem((2, NX, k_dim // 2, own), BF16),
            vmem((2, NY, NX, piece, own), BF16),
            vmem((2, NX, k_dim // 2, own), BF16),
            vmem((2, NY, NX, piece, own), BF16),
            vmem((2, NY, piece, own), BF16),
            vmem((2, NX, piece, own), BF16),
            vmem((2, NY, piece, own), BF16),
            vmem((2, NX, piece, own), BF16),
            vmem((NZ, 16, own // 2), BF16),
            vmem((NZ, 16, own // 2), BF16),
            vmem((NY, NZ, 16, own // 2), BF16),
            vmem((2, k_dim, cols), F32),
            vmem((k_dim, cols), BF16),
            vmem((k_dim, cols), BF16),
            vmem((2, 1, 128), F32),
            vmem((k_dim, own), F32),
            pltpu.SemaphoreType.DMA((160,)),
            pltpu.SemaphoreType.DMA((160,)),
        ]
        loss, grad_student, grad_prototypes = pl.pallas_call(
            functools.partial(kernel, float(total_rows), float(total_cols)),
            out_shape=(
                jax.ShapeDtypeStruct((1, 128), F32),
                jax.ShapeDtypeStruct((own, k_dim), F32),
                jax.ShapeDtypeStruct((k_dim, cols), F32),
            ),
            in_specs=[pl.BlockSpec(memory_space=vmem)] * 3,
            out_specs=[pl.BlockSpec(memory_space=vmem)] * 3,
            scratch_shapes=scratch,
            compiler_params=pltpu.CompilerParams(
                collective_id=0, has_side_effects=True, vmem_limit_bytes=60 << 20
            ),
            name="prototype_head",
        )(teacher_emb, student_emb, prototypes)
        return loss[0, 0], grad_student, grad_prototypes

    in_specs = (P("dp", None), P("dp", None), P(None, ("dp", "proto")))
    out_specs = (P(), P("dp", None), P(None, ("dp", "proto")))
    return jax.shard_map(shards, mesh=mesh, in_specs=in_specs, out_specs=out_specs, check_vma=False)
```

time: 699 us -> 112 us (0.16)
  blocking collectives: 299 us -> 0 us
  waiting for transfers between devices: 288 us -> 0 us
  Pallas kernels: 0 us -> 105 us
  other arithmetic: 58.9 us -> 0 us
  matrix products: 32.3 us -> 0 us
  between operations: 15.7 us -> 2.5 us
    psum x4 -> x0, blocking collectives: 299 us -> none  [the longest x3 224 us: sink_mass(): return lax.psum(partial_sums, ('dp', 'proto'))]
    psum x1 -> x0, waiting for transfers between devices: 255 us -> none  [shards(): embed_all, cross_all = lax.psum((embed_part, cross_part), ('dp', 'proto'))]
    pallas_call x0 -> x1, Pallas kernels: none -> 105 us  [shards(): pl.pallas_call(functools.partial(kernel, float(total_rows), float(total_c...]
    reduce_sum x10 -> x0, other arithmetic: 42.9 us -> none  [the longest x3 21.8 us: shards(): partial_rows = jnp.sum(expo * col_scale[None, :], axis=1)]
    dot_general x4 -> x0, matrix products: 32.3 us -> none  [the longest x1 12.6 us: shards(): jnp.dot(stud_hat, proto_hat, preferred_element_type=jnp.float32)]
    all_gather x2 -> x0, waiting for transfers between devices: 31.9 us -> none  [the longest x1 31.9 us: shards(): lax.all_gather(teacher_emb, 'dp', axis=0, tiled=True)]
    convert_element_type x1 -> x0, other arithmetic: 12.1 us -> none  [shards(): delta = ((probs - targets) / STUDENT_TEMP).astype(jnp.bfloat16)]
  transfers between devices with their start and end apart: 3 -> 0, of which waited for: 2 -> 0; matrix products, arithmetic and copies ran while one was open for 8% -> 0% of each run, Pallas kernels for 0% -> 0%
where the time goes in v1:
time: 112 us; the launch traced here: 110 us
  Pallas kernels  105 us (94%)
  local copies, waits for them, and re-layouts  2.84 us (3%)
  between operations  2.5 us (2%)
    pallas_call x1, Pallas kernels, shards(): pl.pallas_call(functools.partial(kernel, float(total_rows), float(total_c...  105 us
    unnamed x4, local copies, waits for them, and re-layouts  2.84 us

profile of v1, /device:TPU:1, one launch (start us, length us, event | category | flops | bytes accessed | tf_op | source)
XLA Modules:
  0.0 110.1 jit_solution(4859614517045713815)
XLA Ops:
  0.6 104.7 %prototype_head.1 = (f32[1,128]{1,0:T(1,128)}, f32[512,256]{1,0:T(8,128)}, f32[256,1024]{1,0:T(8,128)}) custom-call(bf16[512,256]{1,0:T(8,128)(2,1)} %teach_ref.1, bf16[512,256]{1,0:T(8,128)(2,1)} %stud_ref.1, bf16[256,1024]{1,0:T(8,128)(2,1)} %proto_ref.1), custom_call_target="tpu_custom_call" | custom-call | tf_op jit(solution)/shard_map/prototype_head/pallas_call | solution.py:507
  105.4 0.0 copy-start
  106.1 1.9 %copy.10 = f32[512,256]{1,0:T(8,128)} copy(f32[512,256]{1,0:T(8,128)} %get-tuple-element.13) | data formatting | bytes 1048576
  108.0 0.0 copy-done
  108.0 1.0 copy.11
Async XLA Ops:
  105.4 2.6 %copy-start = (f32[256,1024]{1,0:T(8,128)S(1)}, f32[256,1024]{1,0:T(8,128)}, u32[]{:S(2)}) copy-start(f32[256,1024]{1,0:T(8,128)} %get-tuple-element.14) | copy-start | bytes 3145732

commit v2 on v1

v2 whole, which is shorter than its diff:
```python
import functools
import math

import jax
import jax.numpy as jnp
from jax import lax
from jax.experimental import pallas as pl
from jax.experimental.pallas import tpu as pltpu
from jax.sharding import PartitionSpec as P

ITERS = 3
TEACHER_TEMP = 0.04
STUDENT_TEMP = 0.1
NORM_EPS = 1e-06
LOG2E = 1.4426950408889634
NX, NC, NY, NZ = 4, 2, 4, 8

MESH = pl.DeviceIdType.MESH
scope = jax.named_scope
F32, BF16 = jnp.float32, jnp.bfloat16
NT = (((1,), (1,)), ((), ()))


def unit_along(values, axis):
    floats = values.astype(F32)
    inverse = lax.rsqrt(jnp.sum(floats * floats, axis=axis, keepdims=True) + NORM_EPS)
    return floats * inverse, inverse


def split_rows(vec):
    n = vec.shape[1]
    high = vec.astype(BF16).astype(F32)
    low = vec - high
    row = lax.broadcasted_iota(jnp.int32, (16, n), 0)
    both = jnp.where(row == 0, high, jnp.where(row == 1, low, 0.0))
    return both.astype(BF16)


def kernel(
    total_rows,
    total_cols,
    teach_ref,
    stud_ref,
    proto_ref,
    loss_ref,
    gs_ref,
    gp_ref,
    teach_all,
    stud_all,
    proto_all,
    protot_all,
    left,
    exp_t,
    exp_s,
    acc,
    colx,
    xy_vec,
    z_vec,
    xy_loss,
    z_loss,
    send_a,
    send_b,
    recv_a,
    recv_b,
    send_a2,
    send_b2,
    recv_a2,
    recv_b2,
    zsend,
    zrecv,
    ygather,
    cross,
    fac_mix,
    dw_buf,
    dw_send,
    dw_recv,
    loss_x,
    dzt,
    ssem,
    rsem,
):
    d = lax.axis_index("dp")
    p = lax.axis_index("proto")
    x, c = d // NC, lax.rem(d, NC)
    z, y = p // NY, lax.rem(p, NY)
    own = teach_ref.shape[0]
    k_dim, cols = proto_ref.shape
    rows = NX * own
    both_cols = 2 * cols
    half_own = own // 2

    def at_x(k):
        return lax.rem(x + k, NX)

    def at_y(k):
        return lax.rem(y + k, NY)

    def at_z(k):
        return lax.rem(z + k, NZ)

    def dev(xx, cc, yy, zz):
        return (xx * NC + cc, zz * NY + yy)

    def x_dev(xx):
        return dev(xx, c, y, z)

    def y_dev(yy):
        return dev(x, c, yy, z)

    def z_dev(zz):
        return dev(x, c, y, zz)

    partner = dev(x, 1 - c, y, z)
    xy_peers = [dev(at_x(k // 4), c, at_y(k % 4), z) for k in range(1, 16)]
    z_peers = [z_dev(at_z(k)) for k in range(1, 8)]
    everyone = [partner] + xy_peers + z_peers
    AROUND = (2, 1, 3)

    barrier = pltpu.get_barrier_semaphore()
    for peer in everyone:
        pl.semaphore_signal(barrier, inc=1, device_id=peer, device_id_type=MESH)

    started = []

    def send(src, dst, peer):
        index = len(started)
        copy = pltpu.make_async_remote_copy(
            src_ref=src,
            dst_ref=dst,
            send_sem=ssem.at[index],
            recv_sem=rsem.at[index],
            device_id=peer,
            device_id_type=MESH,
        )
        copy.start()
        started.append(copy)
        return index

    def arrive(index, landed, peer):
        pltpu.make_async_remote_copy(
            src_ref=landed,
            dst_ref=landed,
            send_sem=ssem.at[index],
            recv_sem=rsem.at[index],
            device_id=peer,
            device_id_type=MESH,
        ).wait_recv()

    def start_gather(blocks):
        far = send(blocks.at[x, y], blocks.at[x, y], x_dev(at_x(2)))
        return far, {k: send(blocks.at[x], blocks.at[x], x_dev(at_x(k))) for k in (1, 3)}

    def relay_far(blocks, copies):
        source = at_x(2)
        arrive(copies[0], blocks.at[source, y], x_dev(source))
        return {
            k: send(blocks.at[source, y], blocks.at[source, y], y_dev(at_y(k))) for k in AROUND
        }

    def finish_far(blocks, relays):
        source = at_x(2)
        for k in AROUND:
            sy = at_y(NY - k)
            arrive(relays[k], blocks.at[source, sy], y_dev(sy))

    def block_of(blocks, j):
        return blocks[j].reshape(k_dim, own)

    with scope("s_norm"):
        teach_hat = unit_along(teach_ref[...], 1)[0]
        teach_all[x] = jnp.transpose(teach_hat).astype(BF16).reshape(4, k_dim // 4, own)
    with scope("s_barrier"):
        pl.semaphore_wait(barrier, len(everyone))
    with scope("s_norm"):
        teach_copies = start_gather(teach_all)
        proto_unit = unit_along(proto_ref[...], 0)[0]
        protot_all[c] = jnp.transpose(proto_unit).astype(BF16)
        protot_copy = send(protot_all.at[c], protot_all.at[c], partner)
        proto_all[c] = proto_unit.astype(BF16)
        proto_copy = send(proto_all.at[c], proto_all.at[c], partner)
        stud_hat = unit_along(stud_ref[...], 1)[0]
        stud_all[x] = jnp.transpose(stud_hat).astype(BF16).reshape(4, k_dim // 4, own)
        stud_copies = start_gather(stud_all)

    CH = 512
    half_steps = cols // CH

    def teacher_block(block, half):
        def body(i, carry):
            rows_in = pl.ds(pl.multiple_of(i * CH, CH), CH)
            rows_out = pl.ds(pl.multiple_of(half * cols + i * CH, CH), CH)
            prod = jnp.dot(
                protot_all[half, rows_in, :],
                block_of(teach_all, block),
                preferred_element_type=F32,
            )
            e = jnp.exp2(prod * (LOG2E / TEACHER_TEMP))
            exp_t[block, rows_out, :] = e.astype(BF16)
            part = e[:, 0:128]
            for lane in range(128, own, 128):
                part = part + e[:, lane : lane + 128]
            acc[rows_out, :] += part
            return carry

        lax.fori_loop(0, half_steps, body, 0)

    def student_block(block):
        def body(i, carry):
            half, inner = i // half_steps, lax.rem(i, half_steps)
            prod = jnp.dot(
                protot_all[half, pl.ds(pl.multiple_of(inner * CH, CH), CH), :],
                block_of(stud_all, block),
                preferred_element_type=F32,
            )
            exp_s[block, pl.ds(pl.multiple_of(i * CH, CH), CH), :] = jnp.exp2(
                prod * (LOG2E / STUDENT_TEMP)
            ).astype(BF16)
            return carry

        lax.fori_loop(0, 2 * half_steps, body, 0)

    with scope("s_T_own"):
        acc[...] = jnp.zeros_like(acc)
        teacher_block(x, c)
        arrive(protot_copy, protot_all.at[1 - c], partner)
        teacher_block(x, 1 - c)
    with scope("s_relay"):
        teach_relays = relay_far(teach_all, teach_copies)
    with scope("s_T_near"):
        for k in (1, 3):
            source = at_x(NX - k)
            arrive(teach_copies[1][k], teach_all.at[source], x_dev(source))
            teacher_block(source, 0)
            teacher_block(source, 1)
    with scope("s_relay"):
        stud_relays = relay_far(stud_all, stud_copies)
    with scope("s_T_far_wait"):
        finish_far(teach_all, teach_relays)
    with scope("s_T_far"):
        teacher_block(at_x(2), 0)
        teacher_block(at_x(2), 1)

    def column_scale(step, sums):
        colx[step, c] = sums
        index = send(colx.at[step, c], colx.at[step, c], partner)
        arrive(index, colx.at[step, 1 - c], partner)
        return 1.0 / (total_cols * (colx[step, 0] + colx[step, 1]))

    def first_column_sums():
        parts = []
        for b in range(both_cols // 128):
            t = jnp.transpose(acc[b * 128 : (b + 1) * 128, :])
            parts.append(jnp.sum(t, axis=0, keepdims=True))
        return jnp.concatenate(parts, axis=1)

    def column_sums(row_scale):
        both = split_rows(row_scale)
        total = None
        for j in range(NX):
            part = lax.dot_general(
                both[:, j * own : (j + 1) * own], exp_t[j], NT, preferred_element_type=F32
            )
            total = part if total is None else total + part
        return total[0:1] + total[1:2]

    def row_sums(col_scale):
        both = split_rows(col_scale)
        parts = []
        for j in range(NX):
            part = jnp.dot(both, exp_t[j], preferred_element_type=F32)
            parts.append(part[0:1] + part[1:2])
        return jnp.concatenate(parts, axis=1)

    xy_me = x * NY + y

    def start_xy(buf, vec):
        buf[xy_me] = vec
        return [send(buf.at[xy_me], buf.at[xy_me], peer) for peer in xy_peers]

    def finish_xy(buf, indices):
        for k, index in zip(range(1, 16), indices):
            sx, sy = at_x(NX - k // 4), at_y(NY - k % 4)
            arrive(index, buf.at[sx * NY + sy], dev(sx, c, sy, z))
        total = buf[0]
        for i in range(1, 16):
            total = total + buf[i]
        return total

    def start_z(buf, vec):
        buf[z] = vec
        return [send(buf.at[z], buf.at[z], peer) for peer in z_peers]

    def finish_z(buf, indices):
        for k, index in zip(range(1, 8), indices):
            sz = at_z(NZ - k)
            arrive(index, buf.at[sz], z_dev(sz))
        total = buf[0]
        for i in range(1, 8):
            total = total + buf[i]
        return total

    half_k, piece = k_dim // 2, k_dim // 8

    def put_block(which, j, value):
        low = value.astype(BF16)
        send_a[which, j] = low[:half_k]
        for q in range(NY):
            send_b[which, q, j] = low[half_k + q * piece : half_k + (q + 1) * piece]

    def send_block_a(which, k):
        j = at_x(k)
        return send(send_a.at[which, j], recv_a.at[which, x], x_dev(j))

    def send_block_b(which, k):
        j = at_x(k)
        return {
            h: send(send_b.at[which, at_y(h), j], recv_b.at[which, y, j], y_dev(at_y(h)))
            for h in AROUND
        }

    def start_second(which, a, b):
        recv_a[which, x] = send_a[which, x]
        recv_b[which, y] = send_b[which, y]
        for k in AROUND:
            source = at_x(NX - k)
            arrive(a[k], recv_a.at[which, source], x_dev(source))
        total = recv_a[which, 0].astype(F32)
        for i in range(1, NX):
            total = total + recv_a[which, i].astype(F32)
        low = total.astype(BF16)
        for q in range(NY):
            send_a2[which, q] = low[q * piece : (q + 1) * piece]
        a2 = {
            k: send(send_a2.at[which, at_y(k)], recv_a2.at[which, y], y_dev(at_y(k)))
            for k in AROUND
        }
        for k in b:
            for h in AROUND:
                source = at_y(NY - h)
                arrive(b[k][h], recv_b.at[which, source, at_x(k)], y_dev(source))
        for j in range(NX):
            total = recv_b[which, 0, j].astype(F32)
            for i in range(1, NY):
                total = total + recv_b[which, i, j].astype(F32)
            send_b2[which, j] = total.astype(BF16)
        b2 = {
            k: send(send_b2.at[which, at_x(k)], recv_b2.at[which, x], x_dev(at_x(k)))
            for k in AROUND
        }
        return a2, b2

    def start_third(which, second):
        a2, b2 = second
        recv_a2[which, y] = send_a2[which, y]
        recv_b2[which, x] = send_b2[which, x]
        for k in AROUND:
            source = at_y(NY - k)
            arrive(a2[k], recv_a2.at[which, source], y_dev(source))
        for k in AROUND:
            source = at_x(NX - k)
            arrive(b2[k], recv_b2.at[which, source], x_dev(source))
        low = recv_a2[which, 0].astype(F32)
        high = recv_b2[which, 0].astype(F32)
        for i in range(1, 4):
            low = low + recv_a2[which, i].astype(F32)
            high = high + recv_b2[which, i].astype(F32)
        low, high = low.astype(BF16), high.astype(BF16)
        for q in range(NZ):
            r = 16 * (q // 2)
            s = half_own * (q % 2)
            part = low[r : r + 16] if r < piece else high[r - piece : r - piece + 16]
            zsend[which, q] = part[:, s : s + half_own]
        return [
            send(zsend.at[which, at_z(k)], zrecv.at[which, z], z_dev(at_z(k)))
            for k in range(1, NZ)
        ]

    def finish_third(which, third):
        zrecv[which, z] = zsend[which, z]
        for k in range(1, NZ):
            sz = at_z(NZ - k)
            arrive(third[k - 1], zrecv.at[which, sz], z_dev(sz))
        total = zrecv[which, 0].astype(F32)
        for i in range(1, NZ):
            total = total + zrecv[which, i].astype(F32)
        return total

    with scope("s_col1"):
        scale = column_scale(0, first_column_sums())
    with scope("s_row1"):
        xy_copies = start_xy(xy_vec.at[0], row_sums(scale))
    with scope("s_S_near"):
        student_block(x)
        for k in (1, 3):
            source = at_x(NX - k)
            arrive(stud_copies[1][k], stud_all.at[source], x_dev(source))
            student_block(source)
    with scope("s_xy1"):
        z_copies = start_z(z_vec.at[0], finish_xy(xy_vec.at[0], xy_copies))
    with scope("s_S_far"):
        finish_far(stud_all, stud_relays)
        student_block(at_x(2))
    with scope("s_P1"):
        arrive(proto_copy, proto_all.at[1 - c], partner)
        left[0:k_dim, 0:cols] = proto_all[0]
        left[0:k_dim, cols:] = proto_all[1]
        left[k_dim:, :] = jnp.ones((16, both_cols), BF16)
        stud_sums = []
        for j in range(NX):
            value = jnp.dot(left[...], exp_s[j], preferred_element_type=F32)
            put_block(0, j, value[0:k_dim])
            stud_sums.append(value[k_dim : k_dim + 1])
        stud_xy = start_xy(xy_vec.at[3], jnp.concatenate(stud_sums, axis=1))
    with scope("s_z1"):
        row_scale = 1.0 / (total_rows * finish_z(z_vec.at[0], z_copies))

    with scope("s_col2"):
        sums = column_sums(row_scale)
    with scope("s_colx2"):
        scale = column_scale(1, sums)
    with scope("s_row2"):
        xy_copies = start_xy(xy_vec.at[1], row_sums(scale))
        a1 = {k: send_block_a(0, k) for k in AROUND}
        b1 = {k: send_block_b(0, k) for k in (0, 1, 2, 3)}
    with scope("s_studxy"):
        stud_z = start_z(z_vec.at[3], finish_xy(xy_vec.at[3], stud_xy))
    with scope("s_xy2"):
        z_copies = start_z(z_vec.at[1], finish_xy(xy_vec.at[1], xy_copies))
    with scope("s_second1"):
        second1 = start_second(0, a1, b1)
    with scope("s_z2"):
        row_scale = 1.0 / (total_rows * finish_z(z_vec.at[1], z_copies))

    with scope("s_col3"):
        sums = column_sums(row_scale)
    with scope("s_colx3"):
        scale = column_scale(2, sums)
    with scope("s_P2"):
        for h in range(NC):
            left[0:k_dim, h * cols : (h + 1) * cols] = (
                proto_all[h].astype(F32) * scale[:, h * cols : (h + 1) * cols]
            ).astype(BF16)
        left[k_dim:, :] = split_rows(scale)
        a2, b2 = {}, {}
        for k in (2, 1, 3, 0):
            j = at_x(k)
            value = jnp.dot(left[...], exp_t[j], preferred_element_type=F32)
            put_block(1, j, value[0:k_dim])
            if k:
                a2[k] = send_block_a(1, k)
            b2[k] = send_block_b(1, k)
            xy_vec[2, xy_me, :, pl.ds(pl.multiple_of(j * own, own), own)] = (
                value[k_dim : k_dim + 1] + value[k_dim + 1 : k_dim + 2]
            )
            cross[j] = jnp.sum(
                value[0:k_dim] * block_of(stud_all, j).astype(F32), axis=0, keepdims=True
            )
        xy_copies = [
            send(xy_vec.at[2, xy_me], xy_vec.at[2, xy_me], peer) for peer in xy_peers
        ]
    with scope("s_third1"):
        third1 = start_third(0, second1)

    with scope("s_dwS"):
        stud_total = finish_z(z_vec.at[3], stud_z)
        stud_factor = (1.0 / STUDENT_TEMP) / stud_total
        for h in range(NC):
            total = None
            for j in range(NX):
                weights = (
                    block_of(stud_all, j).astype(F32) * stud_factor[:, j * own : (j + 1) * own]
                ).astype(BF16)
                part = lax.dot_general(
                    weights,
                    exp_s[j, h * cols : (h + 1) * cols, :],
                    NT,
                    preferred_element_type=F32,
                )
                total = part if total is None else total + part
            dw_buf[h] = total
    with scope("s_xy3"):
        z_copies = start_z(z_vec.at[2], finish_xy(xy_vec.at[2], xy_copies))
    with scope("s_second2"):
        second2 = start_second(1, a2, b2)
    with scope("s_third2"):
        third2 = start_third(1, second2)
    with scope("s_z3"):
        row_scale = 1.0 / (total_rows * finish_z(z_vec.at[2], z_copies))
        teach_factor = (total_rows / STUDENT_TEMP) * row_scale

    with scope("s_loss"):
        part = None
        for j in range(NX):
            term = teach_factor[:, j * own : (j + 1) * own] * cross[j]
            for lane in range(0, own, 128):
                t = term[:, lane : lane + 128]
                part = t if part is None else part + t
        loss_xy = start_xy(xy_loss, part)

    with scope("s_mix"):
        part1 = finish_third(0, third1)
        part2 = finish_third(1, third2)
        for i in range(2 * NX):
            s = i * half_own
            fac_mix[0, i] = stud_factor[:, s : s + half_own]
            fac_mix[1, i] = teach_factor[:, s : s + half_own]
        mine = x * 2 + lax.rem(z, 2)
        ygather[y, z] = (fac_mix[0, mine] * part1 - fac_mix[1, mine] * part2).astype(BF16)
        gather_z = [
            send(ygather.at[y, z], ygather.at[y, z], z_dev(at_z(k))) for k in range(1, NZ)
        ]

    with scope("s_dwT"):
        for h in range(NC):
            total = None
            for j in range(NX):
                weights = (
                    block_of(stud_all, j).astype(F32) * teach_factor[:, j * own : (j + 1) * own]
                ).astype(BF16)
                part = lax.dot_general(
                    weights,
                    exp_t[j, h * cols : (h + 1) * cols, :],
                    NT,
                    preferred_element_type=F32,
                )
                total = part if total is None else total + part
            dw_buf[h] = dw_buf[h] - total * scale[:, h * cols : (h + 1) * cols]
        dw_send[...] = dw_buf[1 - c].astype(BF16)
        dw_copy = send(dw_send, dw_recv, partner)
    with scope("s_lossxy"):
        loss_z = start_z(z_loss, finish_xy(xy_loss, loss_xy))
    with scope("s_gatherz"):
        for k in range(1, NZ):
            sz = at_z(NZ - k)
            arrive(gather_z[k - 1], ygather.at[y, sz], z_dev(sz))
        gather_y = {k: send(ygather.at[y], ygather.at[y], y_dev(at_y(k))) for k in AROUND}
    with scope("s_gp"):
        arrive(dw_copy, dw_recv, partner)
        dw_hat = dw_buf[c] + dw_recv[...].astype(F32)
        proto_unit, proto_inverse = unit_along(proto_ref[...], 0)
        gp_ref[...] = (
            (total_cols / math.sqrt(total_rows))
            * proto_inverse
            * (dw_hat - proto_unit * jnp.sum(proto_unit * dw_hat, axis=0, keepdims=True))
        )
    with scope("s_lossz"):
        lse = jnp.log(stud_total)
        part = lse[:, 0:128]
        for lane in range(128, rows, 128):
            part = part + lse[:, lane : lane + 128]
        loss_x[c] = part - finish_z(z_loss, loss_z)
        loss_copy = send(loss_x.at[c], loss_x.at[c], partner)
    with scope("s_gathery"):
        for k in AROUND:
            source = at_y(NY - k)
            arrive(gather_y[k], ygather.at[source], y_dev(source))
    with scope("s_dz"):
        for i in range(NY):
            for q in range(NZ):
                r = 16 * (q // 2)
                s = half_own * (q % 2)
                base = i * piece + r if r < piece else half_k + i * piece + r - piece
                dzt[base : base + 16, s : s + half_own] = ygather[i, q].astype(F32)
        dz = jnp.transpose(dzt[...])
        stud_unit, stud_inverse = unit_along(stud_ref[...], 1)
        gs_ref[...] = stud_inverse * (
            dz - stud_unit * jnp.sum(stud_unit * dz, axis=1, keepdims=True)
        )
    with scope("s_end"):
        arrive(loss_copy, loss_x.at[1 - c], partner)
        loss_ref[...] = jnp.broadcast_to(
            jnp.sum(loss_x[0] + loss_x[1], axis=1, keepdims=True) / total_rows, loss_ref.shape
        )
        for copy in started:
            copy.wait_send()


def solution(mesh):
    def shards(teacher_emb, student_emb, prototypes):
        own, k_dim = teacher_emb.shape
        cols = prototypes.shape[1]
        rows, both = NX * own, 2 * cols
        total_rows = own * mesh.shape["dp"]
        total_cols = cols * mesh.shape["dp"] * mesh.shape["proto"]
        vmem = pltpu.VMEM
        piece = k_dim // 8
        scratch = [
            vmem((NX, 4, k_dim // 4, own), BF16),
            vmem((NX, 4, k_dim // 4, own), BF16),
            vmem((NC, k_dim, cols), BF16),
            vmem((NC, cols, k_dim), BF16),
            vmem((k_dim + 16, both), BF16),
            vmem((NX, both, own), BF16),
            vmem((NX, both, own), BF16),
            vmem((both, 128), F32),
            vmem((ITERS, NC, 1, both), F32),
            vmem((ITERS + 1, NX * NY, 1, rows), F32),
            vmem((ITERS + 1, NZ, 1, rows), F32),
            vmem((NX * NY, 1, 128), F32),
            vmem((NZ, 1, 128), F32),
            vmem((2, NX, k_dim // 2, own), BF16),
            vmem((2, NY, NX, piece, own), BF16),
            vmem((2, NX, k_dim // 2, own), BF16),
            vmem((2, NY, NX, piece, own), BF16),
            vmem((2, NY, piece, own), BF16),
            vmem((2, NX, piece, own), BF16),
            vmem((2, NY, piece, own), BF16),
            vmem((2, NX, piece, own), BF16),
            vmem((2, NZ, 16, own // 2), BF16),
            vmem((2, NZ, 16, own // 2), BF16),
            vmem((NY, NZ, 16, own // 2), BF16),
            vmem((NX, 1, own), F32),
            vmem((2, 2 * NX, 1, own // 2), F32),
            vmem((2, k_dim, cols), F32),
            vmem((k_dim, cols), BF16),
            vmem((k_dim, cols), BF16),
            vmem((2, 1, 128), F32),
            vmem((k_dim, own), F32),
            pltpu.SemaphoreType.DMA((240,)),
            pltpu.SemaphoreType.DMA((240,)),
        ]
        loss, grad_student, grad_prototypes = pl.pallas_call(
            functools.partial(kernel, float(total_rows), float(total_cols)),
            out_shape=(
                jax.ShapeDtypeStruct((1, 128), F32),
                jax.ShapeDtypeStruct((own, k_dim), F32),
                jax.ShapeDtypeStruct((k_dim, cols), F32),
            ),
            in_specs=[pl.BlockSpec(memory_space=vmem)] * 3,
            out_specs=[pl.BlockSpec(memory_space=vmem)] * 3,
            scratch_shapes=scratch,
            compiler_params=pltpu.CompilerParams(
                collective_id=0, has_side_effects=True, vmem_limit_bytes=60 << 20
            ),
            name="prototype_head",
        )(teacher_emb, student_emb, prototypes)
        return loss[0, 0], grad_student, grad_prototypes

    in_specs = (P("dp", None), P("dp", None), P(None, ("dp", "proto")))
    out_specs = (P(), P("dp", None), P(None, ("dp", "proto")))
    return jax.shard_map(shards, mesh=mesh, in_specs=in_specs, out_specs=out_specs, check_vma=False)
```

time: 112 us -> 96.1 us (0.86); the launches traced: 110 us -> 95.9 us
  Pallas kernels: 105 us -> 90.6 us
    pallas_call x1, Pallas kernels: 105 us -> 90.6 us  [shards(): pl.pallas_call(functools.partial(kernel, float(total_rows), float(total_c...]
where the time goes in v2:
time: 96.1 us; the launch traced here: 95.9 us
  Pallas kernels  90.6 us (94%)
  local copies, waits for them, and re-layouts  2.84 us (3%)
  between operations  2.5 us (3%)
    pallas_call x1, Pallas kernels, shards(): pl.pallas_call(functools.partial(kernel, float(total_rows), float(total_c...  90.6 us
    unnamed x4, local copies, waits for them, and re-layouts  2.84 us

profile of v2, /device:TPU:1, one launch (start us, length us, event | category | flops | bytes accessed | tf_op | source)
XLA Modules:
  0.0 95.9 jit_solution(14253185082590304673)
XLA Ops:
  0.6 90.6 %prototype_head.1 = (f32[1,128]{1,0:T(1,128)}, f32[512,256]{1,0:T(8,128)}, f32[256,1024]{1,0:T(8,128)}) custom-call(bf16[512,256]{1,0:T(8,128)(2,1)} %teach_ref.1, bf16[512,256]{1,0:T(8,128)(2,1)} %stud_ref.1, bf16[256,1024]{1,0:T(8,128)(2,1)} %proto_ref.1), custom_call_target="tpu_custom_call" | custom-call | tf_op jit(solution)/shard_map/prototype_head/pallas_call | solution.py:622
  91.2 0.0 copy-start
  92.0 1.9 %copy.10 = f32[512,256]{1,0:T(8,128)} copy(f32[512,256]{1,0:T(8,128)} %get-tuple-element.13) | data formatting | bytes 1048576
  93.8 0.0 copy-done
  93.8 1.0 %copy.11 = f32[256,1024]{1,0:T(8,128)} copy(f32[256,1024]{1,0:T(8,128)S(1)} %copy-done) | data formatting | bytes 2097152
Async XLA Ops:
  91.2 2.6 %copy-start = (f32[256,1024]{1,0:T(8,128)S(1)}, f32[256,1024]{1,0:T(8,128)}, u32[]{:S(2)}) copy-start(f32[256,1024]{1,0:T(8,128)} %get-tuple-element.14) | copy-start | bytes 3145732

commit v3 on v2

v3 whole, which is shorter than its diff:
```python
import functools
import math

import jax
import jax.numpy as jnp
from jax import lax
from jax.experimental import pallas as pl
from jax.experimental.pallas import tpu as pltpu
from jax.sharding import PartitionSpec as P

ITERS = 3
TEACHER_TEMP = 0.04
STUDENT_TEMP = 0.1
NORM_EPS = 1e-06
LOG2E = 1.4426950408889634
NX, NC, NY, NZ = 4, 2, 4, 8
GROUPS = 43

MESH = pl.DeviceIdType.MESH
scope = jax.named_scope
F32, BF16 = jnp.float32, jnp.bfloat16
NT = (((1,), (1,)), ((), ()))


def unit_along(values, axis):
    floats = values.astype(F32)
    inverse = lax.rsqrt(jnp.sum(floats * floats, axis=axis, keepdims=True) + NORM_EPS)
    return floats * inverse, inverse


def split_rows(vec):
    n = vec.shape[1]
    high = vec.astype(BF16).astype(F32)
    low = vec - high
    row = lax.broadcasted_iota(jnp.int32, (16, n), 0)
    both = jnp.where(row == 0, high, jnp.where(row == 1, low, 0.0))
    return both.astype(BF16)


def kernel(
    total_rows,
    total_cols,
    teach_hbm,
    stud_hbm,
    proto_hbm,
    loss_ref,
    gs_ref,
    gp_ref,
    teach_ref,
    stud_ref,
    proto_ref,
    teach_all,
    stud_all,
    proto_all,
    protot_all,
    left,
    exp_t,
    exp_n,
    exp_s,
    acc,
    colx,
    xy_vec,
    z_vec,
    xy_loss,
    z_loss,
    send_a,
    send_b,
    recv_a,
    recv_b,
    send_a2,
    send_b2,
    recv_a2,
    recv_b2,
    zsend,
    zrecv,
    ygather,
    cross,
    fac_mix,
    dw_buf,
    dw_send,
    dw_recv,
    loss_x,
    dzt,
    ssem,
    rsem,
    lsem,
):
    d = lax.axis_index("dp")
    p = lax.axis_index("proto")
    x, c = d // NC, lax.rem(d, NC)
    z, y = p // NY, lax.rem(p, NY)
    own = teach_ref.shape[0]
    k_dim, cols = proto_ref.shape
    rows = NX * own
    both_cols = 2 * cols
    half_own = own // 2

    def at_x(k):
        return lax.rem(x + k, NX)

    def at_y(k):
        return lax.rem(y + k, NY)

    def at_z(k):
        return lax.rem(z + k, NZ)

    def dev(xx, cc, yy, zz):
        return (xx * NC + cc, zz * NY + yy)

    def x_dev(xx):
        return dev(xx, c, y, z)

    def y_dev(yy):
        return dev(x, c, yy, z)

    def z_dev(zz):
        return dev(x, c, y, zz)

    partner = dev(x, 1 - c, y, z)
    xy_peers = [dev(at_x(k // 4), c, at_y(k % 4), z) for k in range(1, 16)]
    z_peers = [z_dev(at_z(k)) for k in range(1, 8)]
    everyone = [partner] + xy_peers + z_peers
    AROUND = (2, 1, 3)

    barrier = pltpu.get_barrier_semaphore()
    for peer in everyone:
        pl.semaphore_signal(barrier, inc=1, device_id=peer, device_id_type=MESH)

    groups = []

    def group(span):
        groups.append(span)
        return len(groups) - 1

    def copy_of(g, src, dst, peer):
        return pltpu.make_async_remote_copy(
            src_ref=src,
            dst_ref=dst,
            send_sem=ssem.at[g],
            recv_sem=rsem.at[g],
            device_id=peer,
            device_id_type=MESH,
        )

    def send(g, src, dst, peer):
        copy_of(g, src, dst, peer).start()

    def send_one(src, dst, peer):
        g = group(src)
        send(g, src, dst, peer)
        return g

    def arrive(g):
        copy_of(g, groups[g], groups[g], partner).wait_recv()

    def local(src, dst, sem):
        copy = pltpu.make_async_copy(src, dst, lsem.at[sem])
        copy.start()
        return copy

    quarter = own // 4

    def put_own(blocks, hat):
        hat_t = jnp.transpose(hat).astype(BF16)
        for q in range(4):
            blocks[x, q] = hat_t[:, q * quarter : (q + 1) * quarter]

    def start_gather(blocks):
        far = send_one(blocks.at[x, y], blocks.at[x, y], x_dev(at_x(2)))
        near = {}
        for k in (1, 3):
            near[k] = send_one(blocks.at[x, y], blocks.at[x, y], x_dev(at_x(k)))
        rest = []
        for t in (1, 2):
            rest.append(group(blocks.at[0, pl.ds(0, 2)]))
            for k in (1, 3):
                q = at_y(t)
                send(rest[-1], blocks.at[x, q], blocks.at[x, q], x_dev(at_x(k)))
        return far, near, *rest

    def relay_far(blocks, copies):
        source = at_x(2)
        arrive(copies[0])
        g = group(blocks.at[0, pl.ds(0, 3)])
        for k in AROUND:
            send(g, blocks.at[source, y], blocks.at[source, y], y_dev(at_y(k)))
        return g

    def relay_near(blocks, copies):
        g = group(blocks.at[0, pl.ds(0, 2)])
        for k in (1, 3):
            source = at_x(NX - k)
            arrive(copies[1][k])
            send(g, blocks.at[source, y], blocks.at[source, y], y_dev(at_y(1)))
        return g

    def block_of(blocks, j):
        return jnp.concatenate([blocks[j, q] for q in range(4)], axis=1)

    def pair_of(blocks, j, pair):
        return jnp.concatenate([blocks[j, q] for q in pair], axis=1)

    with scope("s_load"):
        teach_load = local(teach_hbm, teach_ref, 0)
        proto_load = local(proto_hbm, proto_ref, 1)
        stud_load = local(stud_hbm, stud_ref, 2)
        teach_load.wait()
    with scope("s_norm"):
        put_own(teach_all, unit_along(teach_ref[...], 1)[0])
    with scope("s_barrier"):
        pl.semaphore_wait(barrier, len(everyone))
    with scope("s_norm"):
        teach_copies = start_gather(teach_all)
        proto_load.wait()
        proto_unit = unit_along(proto_ref[...], 0)[0]
        protot_all[c] = jnp.transpose(proto_unit).astype(BF16)
        protot_copy = send_one(protot_all.at[c], protot_all.at[c], partner)
        proto_all[c] = proto_unit.astype(BF16)
        proto_copy = send_one(proto_all.at[c], proto_all.at[c], partner)
        stud_load.wait()
        put_own(stud_all, unit_along(stud_ref[...], 1)[0])
        stud_copies = start_gather(stud_all)

    def lanes_of(q):
        start = q * quarter
        return pl.ds(start if isinstance(q, int) else pl.multiple_of(start, quarter), quarter)

    def teacher_part(block, pair, half=None):
        if half is None:
            protos_t, rows_out = protot_all[...].reshape(both_cols, k_dim), slice(None)
        else:
            protos_t = protot_all[half]
            rows_out = pl.ds(pl.multiple_of(half * cols, cols), cols)
        prod = jnp.dot(protos_t, pair_of(teach_all, block, pair), preferred_element_type=F32)
        e = jnp.exp2(prod * (LOG2E / TEACHER_TEMP))
        low = e.astype(BF16)
        for i, q in enumerate(pair):
            exp_t[block, rows_out, lanes_of(q)] = low[:, i * quarter : (i + 1) * quarter]
        part = e[:, 0:128]
        for lane in range(128, half_own, 128):
            part = part + e[:, lane : lane + 128]
        acc[rows_out, :] += part

    def student_block(block):
        for pair in ((0, 1), (2, 3)):
            prod = jnp.dot(
                protot_all[...].reshape(both_cols, k_dim),
                pair_of(stud_all, block, pair),
                preferred_element_type=F32,
            )
            low = jnp.exp2(prod * (LOG2E / STUDENT_TEMP)).astype(BF16)
            exp_s[block, :, pair[0] * quarter : (pair[1] + 1) * quarter] = low

    with scope("s_T_own"):
        acc[...] = jnp.zeros_like(acc)
        teacher_part(x, (0, 1), c)
        teacher_part(x, (2, 3), c)
        arrive(protot_copy)
        teacher_part(x, (0, 1), 1 - c)
        teacher_part(x, (2, 3), 1 - c)
    with scope("s_relay_far"):
        teach_far = relay_far(teach_all, teach_copies)
    with scope("s_relay_near"):
        teach_near = relay_near(teach_all, teach_copies)
    with scope("s_direct"):
        arrive(teach_copies[2])
    with scope("s_T_early"):
        for k in (1, 3):
            teacher_part(at_x(k), (y, at_y(1)))
    with scope("s_direct"):
        arrive(teach_copies[3])
    with scope("s_relay_wait"):
        arrive(teach_near)
    with scope("s_T_late"):
        for k in (1, 3):
            teacher_part(at_x(k), (at_y(2), at_y(3)))
    with scope("s_far_wait"):
        arrive(teach_far)
    with scope("s_T_far"):
        teacher_part(at_x(2), (0, 1))
        teacher_part(at_x(2), (2, 3))
    with scope("s_stud_relay"):
        stud_far = relay_far(stud_all, stud_copies)
        stud_near = relay_near(stud_all, stud_copies)

    def column_scale(step, sums):
        colx[step, c] = sums
        arrive(send_one(colx.at[step, c], colx.at[step, c], partner))
        return 1.0 / (total_cols * (colx[step, 0] + colx[step, 1]))

    def first_column_sums():
        parts = []
        for b in range(both_cols // 128):
            t = jnp.transpose(acc[b * 128 : (b + 1) * 128, :])
            parts.append(jnp.sum(t, axis=0, keepdims=True))
        return jnp.concatenate(parts, axis=1)

    def column_sums(row_scale):
        both = split_rows(row_scale)
        total = None
        for j in range(NX):
            part = jnp.dot(
                both[:, j * own : (j + 1) * own], exp_n[j], preferred_element_type=F32
            )
            total = part if total is None else total + part
        return total[0:1] + total[1:2]

    def row_sums(col_scale):
        both = split_rows(col_scale)
        parts = []
        for j in range(NX):
            part = jnp.dot(both, exp_t[j], preferred_element_type=F32)
            parts.append(part[0:1] + part[1:2])
        return jnp.concatenate(parts, axis=1)

    xy_me = x * NY + y

    def send_xy(buf):
        g = group(buf.at[pl.ds(0, 15)])
        for peer in xy_peers:
            send(g, buf.at[xy_me], buf.at[xy_me], peer)
        return g

    def start_xy(buf, vec):
        buf[xy_me] = vec
        return send_xy(buf)

    def start_z(buf, vec):
        buf[z] = vec
        g = group(buf.at[pl.ds(0, 7)])
        for peer in z_peers:
            send(g, buf.at[z], buf.at[z], peer)
        return g

    def finish(buf, g):
        arrive(g)
        total = buf[0]
        for i in range(1, buf.shape[0]):
            total = total + buf[i]
        return total

    half_k, piece = k_dim // 2, k_dim // 8

    def put_block(which, j, value):
        low = value.astype(BF16)
        send_a[which, j] = low[:half_k]
        for q in range(NY):
            send_b[which, q, j] = low[half_k + q * piece : half_k + (q + 1) * piece]

    def first_groups(which):
        return (
            group(recv_a.at[which, pl.ds(0, 3)]),
            group(recv_b.at[which, pl.ds(0, 3)]),
        )

    def send_block(which, first, k):
        j = at_x(k)
        if k:
            send(first[0], send_a.at[which, j], recv_a.at[which, x], x_dev(j))
        for h in AROUND:
            send(
                first[1], send_b.at[which, at_y(h), j], recv_b.at[which, y, j], y_dev(at_y(h))
            )

    def start_second(which, first):
        recv_a[which, x] = send_a[which, x]
        recv_b[which, y] = send_b[which, y]
        arrive(first[0])
        total = recv_a[which, 0].astype(F32)
        for i in range(1, NX):
            total = total + recv_a[which, i].astype(F32)
        low = total.astype(BF16)
        for q in range(NY):
            send_a2[which, q] = low[q * piece : (q + 1) * piece]
        a2 = group(recv_a2.at[which, pl.ds(0, 3)])
        for k in AROUND:
            send(a2, send_a2.at[which, at_y(k)], recv_a2.at[which, y], y_dev(at_y(k)))
        arrive(first[1])
        for j in range(NX):
            total = recv_b[which, 0, j].astype(F32)
            for i in range(1, NY):
                total = total + recv_b[which, i, j].astype(F32)
            send_b2[which, j] = total.astype(BF16)
        b2 = group(recv_b2.at[which, pl.ds(0, 3)])
        for k in AROUND:
            send(b2, send_b2.at[which, at_x(k)], recv_b2.at[which, x], x_dev(at_x(k)))
        return a2, b2

    def start_third(which, second):
        a2, b2 = second
        recv_a2[which, y] = send_a2[which, y]
        recv_b2[which, x] = send_b2[which, x]
        arrive(a2)
        arrive(b2)
        low = recv_a2[which, 0].astype(F32)
        high = recv_b2[which, 0].astype(F32)
        for i in range(1, 4):
            low = low + recv_a2[which, i].astype(F32)
            high = high + recv_b2[which, i].astype(F32)
        low, high = low.astype(BF16), high.astype(BF16)
        for q in range(NZ):
            r = 16 * (q // 2)
            s = half_own * (q % 2)
            part = low[r : r + 16] if r < piece else high[r - piece : r - piece + 16]
            zsend[which, q] = part[:, s : s + half_own]
        third = group(zrecv.at[which, pl.ds(0, 7)])
        for k in range(1, NZ):
            send(third, zsend.at[which, at_z(k)], zrecv.at[which, z], z_dev(at_z(k)))
        return third

    def finish_third(which, third):
        zrecv[which, z] = zsend[which, z]
        arrive(third)
        total = zrecv[which, 0].astype(F32)
        for i in range(1, NZ):
            total = total + zrecv[which, i].astype(F32)
        return total

    with scope("s_col1"):
        scale = column_scale(0, first_column_sums())
    with scope("s_row1"):
        xy_copies = start_xy(xy_vec.at[0], row_sums(scale))
    with scope("s_S_own"):
        student_block(x)
    with scope("s_transpose"):
        for j in range(NX):
            for b in range(both_cols // 128):
                for a in range(own // 128):
                    exp_n[j, a * 128 : (a + 1) * 128, b * 128 : (b + 1) * 128] = jnp.transpose(
                        exp_t[j, b * 128 : (b + 1) * 128, a * 128 : (a + 1) * 128]
                    )
    with scope("s_xy1"):
        z_copies = start_z(z_vec.at[0], finish(xy_vec.at[0], xy_copies))
    with scope("s_stud_wait"):
        arrive(stud_copies[2])
        arrive(stud_copies[3])
        arrive(stud_near)
    with scope("s_S_near"):
        for k in (1, 3):
            student_block(at_x(k))
    with scope("s_S_far"):
        arrive(stud_far)
        student_block(at_x(2))
    with scope("s_P1"):
        arrive(proto_copy)
        left[0:k_dim, 0:cols] = proto_all[0]
        left[0:k_dim, cols:] = proto_all[1]
        left[k_dim:, :] = jnp.ones((16, both_cols), BF16)
        stud_sums = []
        for j in range(NX):
            value = jnp.dot(left[...], exp_s[j], preferred_element_type=F32)
            put_block(0, j, value[0:k_dim])
            stud_sums.append(value[k_dim : k_dim + 1])
        stud_xy = start_xy(xy_vec.at[3], jnp.concatenate(stud_sums, axis=1))
    with scope("s_z1"):
        row_scale = 1.0 / (total_rows * finish(z_vec.at[0], z_copies))

    with scope("s_col2"):
        sums = column_sums(row_scale)
    with scope("s_colx2"):
        scale = column_scale(1, sums)
    with scope("s_row2"):
        xy_copies = start_xy(xy_vec.at[1], row_sums(scale))
        first1 = first_groups(0)
        for k in (2, 1, 3, 0):
            send_block(0, first1, k)
    with scope("s_studxy"):
        stud_z = start_z(z_vec.at[3], finish(xy_vec.at[3], stud_xy))
    with scope("s_xy2"):
        z_copies = start_z(z_vec.at[1], finish(xy_vec.at[1], xy_copies))
    with scope("s_second1"):
        second1 = start_second(0, first1)
    with scope("s_z2"):
        row_scale = 1.0 / (total_rows * finish(z_vec.at[1], z_copies))

    with scope("s_col3"):
        sums = column_sums(row_scale)
    with scope("s_colx3"):
        scale = column_scale(2, sums)
    with scope("s_P2"):
        for h in range(NC):
            left[0:k_dim, h * cols : (h + 1) * cols] = (
                proto_all[h].astype(F32) * scale[:, h * cols : (h + 1) * cols]
            ).astype(BF16)
        left[k_dim:, :] = split_rows(scale)
        first2 = first_groups(1)
        for k in (2, 1, 3, 0):
            j = at_x(k)
            value = jnp.dot(left[...], exp_t[j], preferred_element_type=F32)
            put_block(1, j, value[0:k_dim])
            send_block(1, first2, k)
            xy_vec[2, xy_me, :, pl.ds(pl.multiple_of(j * own, own), own)] = (
                value[k_dim : k_dim + 1] + value[k_dim + 1 : k_dim + 2]
            )
            cross[j] = jnp.sum(
                value[0:k_dim] * block_of(stud_all, j).astype(F32), axis=0, keepdims=True
            )
        xy_copies = send_xy(xy_vec.at[2])
    with scope("s_third1"):
        third1 = start_third(0, second1)

    with scope("s_dwS"):
        stud_total = finish(z_vec.at[3], stud_z)
        stud_factor = (1.0 / STUDENT_TEMP) / stud_total
        for h in range(NC):
            total = None
            for j in range(NX):
                weights = (
                    block_of(stud_all, j).astype(F32) * stud_factor[:, j * own : (j + 1) * own]
                ).astype(BF16)
                part = lax.dot_general(
                    weights,
                    exp_s[j, h * cols : (h + 1) * cols, :],
                    NT,
                    preferred_element_type=F32,
                )
                total = part if total is None else total + part
            dw_buf[h] = total
    with scope("s_second2"):
        second2 = start_second(1, first2)
    with scope("s_xy3"):
        z_copies = start_z(z_vec.at[2], finish(xy_vec.at[2], xy_copies))
    with scope("s_third2"):
        third2 = start_third(1, second2)
    with scope("s_z3"):
        row_scale = 1.0 / (total_rows * finish(z_vec.at[2], z_copies))
        teach_factor = (total_rows / STUDENT_TEMP) * row_scale

    with scope("s_loss"):
        part = None
        for j in range(NX):
            term = teach_factor[:, j * own : (j + 1) * own] * cross[j]
            for lane in range(0, own, 128):
                t = term[:, lane : lane + 128]
                part = t if part is None else part + t
        loss_xy = start_xy(xy_loss, part)

    with scope("s_mix"):
        part1 = finish_third(0, third1)
        part2 = finish_third(1, third2)
        for i in range(2 * NX):
            s = i * half_own
            fac_mix[0, i] = stud_factor[:, s : s + half_own]
            fac_mix[1, i] = teach_factor[:, s : s + half_own]
        mine = x * 2 + lax.rem(z, 2)
        ygather[y, z] = (fac_mix[0, mine] * part1 - fac_mix[1, mine] * part2).astype(BF16)
        gather_z = group(ygather.at[0, pl.ds(0, 7)])
        for k in range(1, NZ):
            send(gather_z, ygather.at[y, z], ygather.at[y, z], z_dev(at_z(k)))

    with scope("s_dwT"):
        for h in range(NC):
            total = None
            for j in range(NX):
                weights = (
                    block_of(stud_all, j).astype(F32) * teach_factor[:, j * own : (j + 1) * own]
                ).astype(BF16)
                part = lax.dot_general(
                    weights,
                    exp_t[j, h * cols : (h + 1) * cols, :],
                    NT,
                    preferred_element_type=F32,
                )
                total = part if total is None else total + part
            dw_buf[h] = dw_buf[h] - total * scale[:, h * cols : (h + 1) * cols]
        dw_send[...] = dw_buf[1 - c].astype(BF16)
        dw_copy = send_one(dw_send, dw_recv, partner)
    with scope("s_lossxy"):
        loss_z = start_z(z_loss, finish(xy_loss, loss_xy))
    with scope("s_gatherz"):
        arrive(gather_z)
        gather_y = group(ygather.at[pl.ds(0, 3)])
        for k in AROUND:
            send(gather_y, ygather.at[y], ygather.at[y], y_dev(at_y(k)))
    with scope("s_gp"):
        arrive(dw_copy)
        dw_hat = dw_buf[c] + dw_recv[...].astype(F32)
        proto_unit, proto_inverse = unit_along(proto_ref[...], 0)
        gp_ref[...] = (
            (total_cols / math.sqrt(total_rows))
            * proto_inverse
            * (dw_hat - proto_unit * jnp.sum(proto_unit * dw_hat, axis=0, keepdims=True))
        )
    with scope("s_lossz"):
        lse = jnp.log(stud_total)
        part = lse[:, 0:128]
        for lane in range(128, rows, 128):
            part = part + lse[:, lane : lane + 128]
        loss_x[c] = part - finish(z_loss, loss_z)
        loss_copy = send_one(loss_x.at[c], loss_x.at[c], partner)
    def sent(some):
        for g in some:
            copy_of(g, groups[g], groups[g], partner).wait_send()

    with scope("s_sent"):
        early = [g for g in range(len(groups)) if g not in (gather_y, loss_copy)]
        sent(early)
    with scope("s_gathery"):
        arrive(gather_y)
    with scope("s_dz"):
        for i in range(NY):
            for q in range(NZ):
                r = 16 * (q // 2)
                s = half_own * (q % 2)
                base = i * piece + r if r < piece else half_k + i * piece + r - piece
                dzt[base : base + 16, s : s + half_own] = ygather[i, q].astype(F32)
        dz = jnp.transpose(dzt[...])
        stud_unit, stud_inverse = unit_along(stud_ref[...], 1)
        gs_ref[...] = stud_inverse * (
            dz - stud_unit * jnp.sum(stud_unit * dz, axis=1, keepdims=True)
        )
    with scope("s_end"):
        arrive(loss_copy)
        loss_ref[...] = jnp.broadcast_to(
            jnp.sum(loss_x[0] + loss_x[1], axis=1, keepdims=True) / total_rows, loss_ref.shape
        )
        assert len(groups) == GROUPS, len(groups)
        sent((gather_y, loss_copy))


def store_kernel(*refs):
    results, outs, sem = refs[:3], refs[3:6], refs[6]
    for i, (result, out) in enumerate(zip(results, outs)):
        pltpu.make_async_copy(result, out, sem.at[i]).start()
    for i, (result, out) in enumerate(zip(results, outs)):
        pltpu.make_async_copy(result, out, sem.at[i]).wait()


def solution(mesh):
    def shards(teacher_emb, student_emb, prototypes):
        own, k_dim = teacher_emb.shape
        cols = prototypes.shape[1]
        rows, both = NX * own, 2 * cols
        total_rows = own * mesh.shape["dp"]
        total_cols = cols * mesh.shape["dp"] * mesh.shape["proto"]
        vmem = pltpu.VMEM
        piece = k_dim // 8
        scratch = [
            vmem((own, k_dim), BF16),
            vmem((own, k_dim), BF16),
            vmem((k_dim, cols), BF16),
            vmem((NX, 4, k_dim, own // 4), BF16),
            vmem((NX, 4, k_dim, own // 4), BF16),
            vmem((NC, k_dim, cols), BF16),
            vmem((NC, cols, k_dim), BF16),
            vmem((k_dim + 16, both), BF16),
            vmem((NX, both, own), BF16),
            vmem((NX, own, both), BF16),
            vmem((NX, both, own), BF16),
            vmem((both, 128), F32),
            vmem((ITERS, NC, 1, both), F32),
            vmem((ITERS + 1, NX * NY, 1, rows), F32),
            vmem((ITERS + 1, NZ, 1, rows), F32),
            vmem((NX * NY, 1, 128), F32),
            vmem((NZ, 1, 128), F32),
            vmem((2, NX, k_dim // 2, own), BF16),
            vmem((2, NY, NX, piece, own), BF16),
            vmem((2, NX, k_dim // 2, own), BF16),
            vmem((2, NY, NX, piece, own), BF16),
            vmem((2, NY, piece, own), BF16),
            vmem((2, NX, piece, own), BF16),
            vmem((2, NY, piece, own), BF16),
            vmem((2, NX, piece, own), BF16),
            vmem((2, NZ, 16, own // 2), BF16),
            vmem((2, NZ, 16, own // 2), BF16),
            vmem((NY, NZ, 16, own // 2), BF16),
            vmem((NX, 1, own), F32),
            vmem((2, 2 * NX, 1, own // 2), F32),
            vmem((2, k_dim, cols), F32),
            vmem((k_dim, cols), BF16),
            vmem((k_dim, cols), BF16),
            vmem((2, 1, 128), F32),
            vmem((k_dim, own), F32),
            pltpu.SemaphoreType.DMA((GROUPS,)),
            pltpu.SemaphoreType.DMA((GROUPS,)),
            pltpu.SemaphoreType.DMA((3,)),
        ]
        anywhere = pl.BlockSpec(memory_space=pl.ANY)
        in_vmem = pl.BlockSpec(memory_space=vmem)
        shapes = ((1, 128), (own, k_dim), (k_dim, cols))
        results = pl.pallas_call(
            functools.partial(kernel, float(total_rows), float(total_cols)),
            out_shape=tuple(vmem(shape, F32) for shape in shapes),
            in_specs=[anywhere] * 3,
            out_specs=[in_vmem] * 3,
            scratch_shapes=scratch,
            compiler_params=pltpu.CompilerParams(
                collective_id=0, has_side_effects=True, vmem_limit_bytes=60 << 20
            ),
            name="prototype_head",
        )(teacher_emb, student_emb, prototypes)
        loss, grad_student, grad_prototypes = pl.pallas_call(
            store_kernel,
            out_shape=tuple(jax.ShapeDtypeStruct(shape, F32) for shape in shapes),
            in_specs=[in_vmem] * 3,
            out_specs=[anywhere] * 3,
            scratch_shapes=[pltpu.SemaphoreType.DMA((3,))],
            name="store_results",
        )(*(pltpu.with_memory_space_constraint(result, vmem) for result in results))
        return loss[0, 0], grad_student, grad_prototypes

    in_specs = (P("dp", None), P("dp", None), P(None, ("dp", "proto")))
    out_specs = (P(), P("dp", None), P(None, ("dp", "proto")))
    return jax.shard_map(shards, mesh=mesh, in_specs=in_specs, out_specs=out_specs, check_vma=False)
```

time: 96.1 us -> 82.8 us (0.86)
  Pallas kernels: 90.6 us -> 81.9 us
  local copies, waits for them, and re-layouts: 2.84 us -> 0 us
  between operations: 2.5 us -> 0.8 us
    pallas_call x1, Pallas kernels: 90.6 us -> 80.7 us  [shards(): pl.pallas_call(functools.partial(kernel, float(total_rows), float(total_c...]
    unnamed x4 -> x0, local copies, waits for them, and re-layouts: 2.84 us -> none
    pallas_call x0 -> x1, Pallas kernels: none -> 1.18 us  [shards(): pl.pallas_call(store_kernel, out_shape=tuple((jax.ShapeDtypeStruct(shape,...]
where the time goes in v3:
time: 82.8 us; the launch traced here: 82.7 us
  Pallas kernels  81.9 us (99%)
    pallas_call x1, Pallas kernels, shards(): pl.pallas_call(functools.partial(kernel, float(total_rows), float(total_c...  80.7 us

profile of v3, /device:TPU:1, one launch (start us, length us, event | category | flops | bytes accessed | tf_op | source)
XLA Modules:
  0.0 82.7 jit_solution(6202842209759049530)
XLA Ops:
  0.6 80.7 %prototype_head.1 = (f32[1,128]{1,0:T(1,128)S(1)}, f32[512,256]{1,0:T(8,128)S(1)}, f32[256,1024]{1,0:T(8,128)S(1)}) custom-call(bf16[512,256]{1,0:T(8,128)(2,1)} %teach_hbm.1, bf16[512,256]{1,0:T(8,128)(2,1)} %stud_hbm.1, bf16[256,1024]{1,0:T(8,128)(2,1)} %proto_hbm.1), custom_call_target="tpu_custom_call" | custom-call | tf_op jit(solution)/shard_map/prototype_head/pallas_call | solution.py:681
  81.4 1.2 %store_results.1 = (f32[1,128]{1,0:T(1,128)}, f32[512,256]{1,0:T(8,128)}, f32[256,1024]{1,0:T(8,128)}) custom-call(f32[1,128]{1,0:T(1,128)S(1)} %get-tuple-element.9.refs_0_, f32[512,256]{1,0:T(8,128)S(1)} %get-tuple-element.10.refs_1_, f32[256,1024]{1,0:T(8,128)S(1)} %get-tuple-element.11.refs_2_), custom_call_target="tpu_custom_call" | custom-call | tf_op jit(solution)/shard_map/store_results/pallas_call | solution.py:692

commit v4 on v3

--- a/solution.py
+++ b/solution.py
@@ -14,7 +14,7 @@
 NORM_EPS = 1e-06
 LOG2E = 1.4426950408889634
 NX, NC, NY, NZ = 4, 2, 4, 8
-GROUPS = 43
+GROUPS = 42
 
 MESH = pl.DeviceIdType.MESH
 scope = jax.named_scope
@@ -65,6 +65,10 @@
     z_loss,
     send_a,
     send_b,
+    far_a,
+    far_b,
+    sum_a,
+    sum_b,
     recv_a,
     recv_b,
     send_a2,
@@ -167,16 +171,14 @@
 
     def start_gather(blocks):
         far = send_one(blocks.at[x, y], blocks.at[x, y], x_dev(at_x(2)))
-        near = {}
-        for k in (1, 3):
-            near[k] = send_one(blocks.at[x, y], blocks.at[x, y], x_dev(at_x(k)))
-        rest = []
-        for t in (1, 2):
-            rest.append(group(blocks.at[0, pl.ds(0, 2)]))
-            for k in (1, 3):
-                q = at_y(t)
-                send(rest[-1], blocks.at[x, q], blocks.at[x, q], x_dev(at_x(k)))
-        return far, near, *rest
+        near = []
+        for pair in ((0, 1), (2, 3)):
+            near.append(group(blocks.at[0, pl.ds(0, 4)]))
+            for t in pair:
+                for k in (1, 3):
+                    q = at_y(t)
+                    send(near[-1], blocks.at[x, q], blocks.at[x, q], x_dev(at_x(k)))
+        return far, *near
 
     def relay_far(blocks, copies):
         source = at_x(2)
@@ -184,14 +186,6 @@
         g = group(blocks.at[0, pl.ds(0, 3)])
         for k in AROUND:
             send(g, blocks.at[source, y], blocks.at[source, y], y_dev(at_y(k)))
-        return g
-
-    def relay_near(blocks, copies):
-        g = group(blocks.at[0, pl.ds(0, 2)])
-        for k in (1, 3):
-            source = at_x(NX - k)
-            arrive(copies[1][k])
-            send(g, blocks.at[source, y], blocks.at[source, y], y_dev(at_y(1)))
         return g
 
     def block_of(blocks, j):
@@ -260,17 +254,13 @@
         teacher_part(x, (2, 3), 1 - c)
     with scope("s_relay_far"):
         teach_far = relay_far(teach_all, teach_copies)
-    with scope("s_relay_near"):
-        teach_near = relay_near(teach_all, teach_copies)
     with scope("s_direct"):
-        arrive(teach_copies[2])
+        arrive(teach_copies[1])
     with scope("s_T_early"):
         for k in (1, 3):
             teacher_part(at_x(k), (y, at_y(1)))
     with scope("s_direct"):
-        arrive(teach_copies[3])
-    with scope("s_relay_wait"):
-        arrive(teach_near)
+        arrive(teach_copies[2])
     with scope("s_T_late"):
         for k in (1, 3):
             teacher_part(at_x(k), (at_y(2), at_y(3)))
@@ -281,12 +271,17 @@
         teacher_part(at_x(2), (2, 3))
     with scope("s_stud_relay"):
         stud_far = relay_far(stud_all, stud_copies)
-        stud_near = relay_near(stud_all, stud_copies)
+
+    def start_column_scale(step, sums):
+        colx[step, c] = sums
+        return send_one(colx.at[step, c], colx.at[step, c], partner)
+
+    def finish_column_scale(step, g):
+        arrive(g)
+        return 1.0 / (total_cols * (colx[step, 0] + colx[step, 1]))
 
     def column_scale(step, sums):
-        colx[step, c] = sums
-        arrive(send_one(colx.at[step, c], colx.at[step, c], partner))
-        return 1.0 / (total_cols * (colx[step, 0] + colx[step, 1]))
+        return finish_column_scale(step, start_column_scale(step, sums))
 
     def first_column_sums():
         parts = []
@@ -325,12 +320,15 @@
         buf[xy_me] = vec
         return send_xy(buf)
 
-    def start_z(buf, vec):
-        buf[z] = vec
+    def send_z(buf):
         g = group(buf.at[pl.ds(0, 7)])
         for peer in z_peers:
             send(g, buf.at[z], buf.at[z], peer)
         return g
+
+    def start_z(buf, vec):
+        buf[z] = vec
+        return send_z(buf)
 
     def finish(buf, g):
         arrive(g)
@@ -343,44 +341,63 @@
 
     def put_block(which, j, value):
         low = value.astype(BF16)
-        send_a[which, j] = low[:half_k]
+        for h in range(2):
+            send_a[which, j, h] = low[h * half_k // 2 : (h + 1) * half_k // 2]
         for q in range(NY):
-            send_b[which, q, j] = low[half_k + q * piece : half_k + (q + 1) * piece]
+            for h in range(2):
+                r = half_k + q * piece + h * piece // 2
+                send_b[which, q, h, j] = low[r : r + piece // 2]
 
     def first_groups(which):
-        return (
-            group(recv_a.at[which, pl.ds(0, 3)]),
-            group(recv_b.at[which, pl.ds(0, 3)]),
-        )
+        refs = (far_a, recv_a, far_b, recv_b)
+        return [group(ref.at[which]) for ref in refs]
 
     def send_block(which, first, k):
         j = at_x(k)
-        if k:
-            send(first[0], send_a.at[which, j], recv_a.at[which, x], x_dev(j))
-        for h in AROUND:
-            send(
-                first[1], send_b.at[which, at_y(h), j], recv_b.at[which, y, j], y_dev(at_y(h))
-            )
+        if k == 2:
+            send(first[0], send_a.at[which, j, 0], far_a.at[which, 0], x_dev(at_x(1)))
+            send(first[0], send_a.at[which, j, 1], far_a.at[which, 1], x_dev(at_x(3)))
+        if k == 1:
+            send(first[1], send_a.at[which, j, 1], recv_a.at[which, 0, 1], x_dev(j))
+        if k == 3:
+            send(first[1], send_a.at[which, j, 0], recv_a.at[which, 1, 0], x_dev(j))
+        up, down, far = at_y(1), at_y(3), at_y(2)
+        send(first[2], send_b.at[which, far, 0, j], far_b.at[which, 0, j], y_dev(up))
+        send(first[2], send_b.at[which, far, 1, j], far_b.at[which, 1, j], y_dev(down))
+        send(first[3], send_b.at[which, up, 1, j], recv_b.at[which, 0, 1, j], y_dev(up))
+        send(first[3], send_b.at[which, down, 0, j], recv_b.at[which, 1, 0, j], y_dev(down))
+
+    def pass_on_a(which, first):
+        arrive(first[0])
+        for h, k in ((0, 1), (1, 3)):
+            both = send_a[which, at_x(k), h].astype(F32) + far_a[which, h].astype(F32)
+            sum_a[which, h] = both.astype(BF16)
+            send(first[1], sum_a.at[which, h], recv_a.at[which, h, h], x_dev(at_x(k)))
+
+    def pass_on_b(which, first):
+        arrive(first[2])
+        for h, k in ((0, 1), (1, 3)):
+            both = send_b[which, at_y(k), h].astype(F32) + far_b[which, h].astype(F32)
+            sum_b[which, h] = both.astype(BF16)
+            send(first[3], sum_b.at[which, h], recv_b.at[which, h, h], y_dev(at_y(k)))
 
     def start_second(which, first):
-        recv_a[which, x] = send_a[which, x]
-        recv_b[which, y] = send_b[which, y]
-        arrive(first[0])
-        total = recv_a[which, 0].astype(F32)
-        for i in range(1, NX):
+        arrive(first[1])
+        total = send_a[which, x].astype(F32)
+        for i in range(2):
             total = total + recv_a[which, i].astype(F32)
-        low = total.astype(BF16)
+        low = total.astype(BF16).reshape(half_k, own)
         for q in range(NY):
             send_a2[which, q] = low[q * piece : (q + 1) * piece]
         a2 = group(recv_a2.at[which, pl.ds(0, 3)])
         for k in AROUND:
             send(a2, send_a2.at[which, at_y(k)], recv_a2.at[which, y], y_dev(at_y(k)))
-        arrive(first[1])
+        arrive(first[3])
         for j in range(NX):
-            total = recv_b[which, 0, j].astype(F32)
-            for i in range(1, NY):
-                total = total + recv_b[which, i, j].astype(F32)
-            send_b2[which, j] = total.astype(BF16)
+            total = send_b[which, y, :, j].astype(F32)
+            for i in range(2):
+                total = total + recv_b[which, i, :, j].astype(F32)
+            send_b2[which, j] = total.astype(BF16).reshape(piece, own)
         b2 = group(recv_b2.at[which, pl.ds(0, 3)])
         for k in AROUND:
             send(b2, send_b2.at[which, at_x(k)], recv_b2.at[which, x], x_dev(at_x(k)))
@@ -429,15 +446,14 @@
                     exp_n[j, a * 128 : (a + 1) * 128, b * 128 : (b + 1) * 128] = jnp.transpose(
                         exp_t[j, b * 128 : (b + 1) * 128, a * 128 : (a + 1) * 128]
                     )
+    with scope("s_stud_wait"):
+        arrive(stud_copies[1])
+        arrive(stud_copies[2])
+        student_block(at_x(1))
     with scope("s_xy1"):
         z_copies = start_z(z_vec.at[0], finish(xy_vec.at[0], xy_copies))
-    with scope("s_stud_wait"):
-        arrive(stud_copies[2])
-        arrive(stud_copies[3])
-        arrive(stud_near)
     with scope("s_S_near"):
-        for k in (1, 3):
-            student_block(at_x(k))
+        student_block(at_x(3))
     with scope("s_S_far"):
         arrive(stud_far)
         student_block(at_x(2))
@@ -468,15 +484,18 @@
         stud_z = start_z(z_vec.at[3], finish(xy_vec.at[3], stud_xy))
     with scope("s_xy2"):
         z_copies = start_z(z_vec.at[1], finish(xy_vec.at[1], xy_copies))
-    with scope("s_second1"):
-        second1 = start_second(0, first1)
+    with scope("s_pass1"):
+        pass_on_a(0, first1)
+        pass_on_b(0, first1)
     with scope("s_z2"):
         row_scale = 1.0 / (total_rows * finish(z_vec.at[1], z_copies))
 
     with scope("s_col3"):
         sums = column_sums(row_scale)
     with scope("s_colx3"):
-        scale = column_scale(2, sums)
+        col_copy = start_column_scale(2, sums)
+        second1 = start_second(0, first1)
+        scale = finish_column_scale(2, col_copy)
     with scope("s_P2"):
         for h in range(NC):
             left[0:k_dim, h * cols : (h + 1) * cols] = (
@@ -489,15 +508,24 @@
             value = jnp.dot(left[...], exp_t[j], preferred_element_type=F32)
             put_block(1, j, value[0:k_dim])
             send_block(1, first2, k)
-            xy_vec[2, xy_me, :, pl.ds(pl.multiple_of(j * own, own), own)] = (
+            z_vec[2, z, :, pl.ds(pl.multiple_of(j * own, own), own)] = (
                 value[k_dim : k_dim + 1] + value[k_dim + 1 : k_dim + 2]
             )
             cross[j] = jnp.sum(
                 value[0:k_dim] * block_of(stud_all, j).astype(F32), axis=0, keepdims=True
             )
-        xy_copies = send_xy(xy_vec.at[2])
+        z_copies = send_z(z_vec.at[2])
+    with scope("s_pass2a"):
+        pass_on_a(1, first2)
     with scope("s_third1"):
         third1 = start_third(0, second1)
+    with scope("s_pass2b"):
+        pass_on_b(1, first2)
+
+    with scope("s_second2"):
+        second2 = start_second(1, first2)
+    with scope("s_z3"):
+        xy_copies = start_xy(xy_vec.at[2], finish(z_vec.at[2], z_copies))
 
     with scope("s_dwS"):
         stud_total = finish(z_vec.at[3], stud_z)
@@ -516,14 +544,10 @@
                 )
                 total = part if total is None else total + part
             dw_buf[h] = total
-    with scope("s_second2"):
-        second2 = start_second(1, first2)
-    with scope("s_xy3"):
-        z_copies = start_z(z_vec.at[2], finish(xy_vec.at[2], xy_copies))
     with scope("s_third2"):
         third2 = start_third(1, second2)
-    with scope("s_z3"):
-        row_scale = 1.0 / (total_rows * finish(z_vec.at[2], z_copies))
+    with scope("s_xy3"):
+        row_scale = 1.0 / (total_rows * finish(xy_vec.at[2], xy_copies))
         teach_factor = (total_rows / STUDENT_TEMP) * row_scale
 
     with scope("s_loss"):
@@ -544,34 +568,48 @@
             fac_mix[1, i] = teach_factor[:, s : s + half_own]
         mine = x * 2 + lax.rem(z, 2)
         ygather[y, z] = (fac_mix[0, mine] * part1 - fac_mix[1, mine] * part2).astype(BF16)
-        gather_z = group(ygather.at[0, pl.ds(0, 7)])
-        for k in range(1, NZ):
-            send(gather_z, ygather.at[y, z], ygather.at[y, z], z_dev(at_z(k)))
+        NEAR, FAR = (1, 7, 2, 6), (3, 5, 4)
+        gather_near = group(ygather.at[0, pl.ds(0, len(NEAR))])
+        gather_far = group(ygather.at[0, pl.ds(0, len(FAR))])
+        for g, steps in ((gather_far, FAR), (gather_near, NEAR)):
+            for k in steps:
+                send(g, ygather.at[y, z], ygather.at[y, z], z_dev(at_z(k)))
+        gather_y = group(ygather.at[pl.ds(0, 3)])
+
+        def forward(steps):
+            for k in steps:
+                sz = at_z(k)
+                for h in AROUND:
+                    send(gather_y, ygather.at[y, sz], ygather.at[y, sz], y_dev(at_y(h)))
+
+    def teacher_half(h):
+        total = None
+        for j in range(NX):
+            weights = (
+                block_of(stud_all, j).astype(F32) * teach_factor[:, j * own : (j + 1) * own]
+            ).astype(BF16)
+            part = lax.dot_general(
+                weights,
+                exp_t[j, h * cols : (h + 1) * cols, :],
+                NT,
+                preferred_element_type=F32,
+            )
+            total = part if total is None else total + part
+        dw_buf[h] = dw_buf[h] - total * scale[:, h * cols : (h + 1) * cols]
 
     with scope("s_dwT"):
-        for h in range(NC):
-            total = None
-            for j in range(NX):
-                weights = (
-                    block_of(stud_all, j).astype(F32) * teach_factor[:, j * own : (j + 1) * own]
-                ).astype(BF16)
-                part = lax.dot_general(
-                    weights,
-                    exp_t[j, h * cols : (h + 1) * cols, :],
-                    NT,
-                    preferred_element_type=F32,
-                )
-                total = part if total is None else total + part
-            dw_buf[h] = dw_buf[h] - total * scale[:, h * cols : (h + 1) * cols]
+        teacher_half(0)
+    with scope("s_lossxy"):
+        loss_z = start_z(z_loss, finish(xy_loss, loss_xy))
+    with scope("s_dwT"):
+        teacher_half(1)
         dw_send[...] = dw_buf[1 - c].astype(BF16)
         dw_copy = send_one(dw_send, dw_recv, partner)
-    with scope("s_lossxy"):
-        loss_z = start_z(z_loss, finish(xy_loss, loss_xy))
     with scope("s_gatherz"):
-        arrive(gather_z)
-        gather_y = group(ygather.at[pl.ds(0, 3)])
-        for k in AROUND:
-            send(gather_y, ygather.at[y], ygather.at[y], y_dev(at_y(k)))
+        arrive(gather_near)
+        forward((0, *NEAR))
+        arrive(gather_far)
+        forward(FAR)
     with scope("s_gp"):
         arrive(dw_copy)
         dw_hat = dw_buf[c] + dw_recv[...].astype(F32)
@@ -653,10 +691,14 @@
             vmem((ITERS + 1, NZ, 1, rows), F32),
             vmem((NX * NY, 1, 128), F32),
             vmem((NZ, 1, 128), F32),
-            vmem((2, NX, k_dim // 2, own), BF16),
-            vmem((2, NY, NX, piece, own), BF16),
-            vmem((2, NX, k_dim // 2, own), BF16),
-            vmem((2, NY, NX, piece, own), BF16),
+            vmem((2, NX, 2, k_dim // 4, own), BF16),
+            vmem((2, NY, 2, NX, piece // 2, own), BF16),
+            vmem((2, 2, k_dim // 4, own), BF16),
+            vmem((2, 2, NX, piece // 2, own), BF16),
+            vmem((2, 2, k_dim // 4, own), BF16),
+            vmem((2, 2, NX, piece // 2, own), BF16),
+            vmem((2, 2, 2, k_dim // 4, own), BF16),
+            vmem((2, 2, 2, NX, piece // 2, own), BF16),
             vmem((2, NY, piece, own), BF16),
             vmem((2, NX, piece, own), BF16),
             vmem((2, NY, piece, own), BF16),

time: 82.8 us -> 80 us (0.966)
  Pallas kernels: 81.9 us -> 78.7 us
    pallas_call x1, Pallas kernels: 80.7 us -> 77.5 us  [shards(): pl.pallas_call(functools.partial(kernel, float(total_rows), float(total_c...]
where the time goes in v4:
time: 80 us; the launch traced here: 79.5 us
  Pallas kernels  78.7 us (98%)
  between operations  0.8 us (1%)
    pallas_call x1, Pallas kernels, shards(): pl.pallas_call(functools.partial(kernel, float(total_rows), float(total_c...  77.5 us

profile of v4, /device:TPU:1, one launch (start us, length us, event | category | flops | bytes accessed | tf_op | source)
XLA Modules:
  0.0 79.5 jit_solution(4318074239549396139)
XLA Ops:
  0.6 77.5 %prototype_head.1 = (f32[1,128]{1,0:T(1,128)S(1)}, f32[512,256]{1,0:T(8,128)S(1)}, f32[256,1024]{1,0:T(8,128)S(1)}) custom-call(bf16[512,256]{1,0:T(8,128)(2,1)} %teach_hbm.1, bf16[512,256]{1,0:T(8,128)(2,1)} %stud_hbm.1, bf16[256,1024]{1,0:T(8,128)(2,1)} %proto_hbm.1), custom_call_target="tpu_custom_call" | custom-call | tf_op jit(solution)/shard_map/prototype_head/pallas_call | solution.py:723
  78.1 1.2 %store_results.1 = (f32[1,128]{1,0:T(1,128)}, f32[512,256]{1,0:T(8,128)}, f32[256,1024]{1,0:T(8,128)}) custom-call(f32[1,128]{1,0:T(1,128)S(1)} %get-tuple-element.9.refs_0_, f32[512,256]{1,0:T(8,128)S(1)} %get-tuple-element.10.refs_1_, f32[256,1024]{1,0:T(8,128)S(1)} %get-tuple-element.11.refs_2_), custom_call_target="tpu_custom_call" | custom-call | tf_op jit(solution)/shard_map/store_results/pallas_call | solution.py:734

commit v5 on v4

--- a/solution.py
+++ b/solution.py
@@ -14,7 +14,7 @@
 NORM_EPS = 1e-06
 LOG2E = 1.4426950408889634
 NX, NC, NY, NZ = 4, 2, 4, 8
-GROUPS = 42
+GROUPS = 50
 
 MESH = pl.DeviceIdType.MESH
 scope = jax.named_scope
@@ -46,10 +46,9 @@
     loss_ref,
     gs_ref,
     gp_ref,
-    teach_ref,
     stud_ref,
     proto_ref,
-    teach_all,
+    teach_raw,
     stud_all,
     proto_all,
     protot_all,
@@ -93,7 +92,7 @@
     p = lax.axis_index("proto")
     x, c = d // NC, lax.rem(d, NC)
     z, y = p // NY, lax.rem(p, NY)
-    own = teach_ref.shape[0]
+    own = stud_ref.shape[0]
     k_dim, cols = proto_ref.shape
     rows = NX * own
     both_cols = 2 * cols
@@ -169,16 +168,27 @@
         for q in range(4):
             blocks[x, q] = hat_t[:, q * quarter : (q + 1) * quarter]
 
-    def start_gather(blocks):
-        far = send_one(blocks.at[x, y], blocks.at[x, y], x_dev(at_x(2)))
-        near = []
-        for pair in ((0, 1), (2, 3)):
-            near.append(group(blocks.at[0, pl.ds(0, 4)]))
-            for t in pair:
-                for k in (1, 3):
-                    q = at_y(t)
-                    send(near[-1], blocks.at[x, q], blocks.at[x, q], x_dev(at_x(k)))
-        return far, *near
+    def start_gather(source, blocks):
+        far = send_one(source.at[y], blocks.at[x, y], x_dev(at_x(2)))
+        mine = 2 + lax.rem(z, 2)
+        first = {
+            k: send_one(source.at[mine], blocks.at[x, mine], x_dev(at_x(k))) for k in (1, 3)
+        }
+        rest = []
+        for q in (0, 1):
+            rest.append(group(blocks.at[0, pl.ds(0, 2)]))
+            for k in (1, 3):
+                send(rest[q], source.at[q], blocks.at[x, q], x_dev(at_x(k)))
+        return far, first, *rest
+
+    def relay_near(blocks, copies):
+        mine = 2 + lax.rem(z, 2)
+        g = group(blocks.at[0, pl.ds(0, 2)])
+        for k, to in ((1, 1), (3, NZ - 1)):
+            source = at_x(NX - k)
+            arrive(copies[1][k])
+            send(g, blocks.at[source, mine], blocks.at[source, mine], z_dev(at_z(to)))
+        return g
 
     def relay_far(blocks, copies):
         source = at_x(2)
@@ -194,17 +204,13 @@
     def pair_of(blocks, j, pair):
         return jnp.concatenate([blocks[j, q] for q in pair], axis=1)
 
-    with scope("s_load"):
-        teach_load = local(teach_hbm, teach_ref, 0)
-        proto_load = local(proto_hbm, proto_ref, 1)
-        stud_load = local(stud_hbm, stud_ref, 2)
-        teach_load.wait()
-    with scope("s_norm"):
-        put_own(teach_all, unit_along(teach_ref[...], 1)[0])
+    teach_load = local(teach_hbm, teach_raw.at[x], 0)
+    proto_load = local(proto_hbm, proto_ref, 1)
+    stud_load = local(stud_hbm, stud_ref, 2)
     with scope("s_barrier"):
         pl.semaphore_wait(barrier, len(everyone))
     with scope("s_norm"):
-        teach_copies = start_gather(teach_all)
+        teach_copies = start_gather(teach_hbm, teach_raw)
         proto_load.wait()
         proto_unit = unit_along(proto_ref[...], 0)[0]
         protot_all[c] = jnp.transpose(proto_unit).astype(BF16)
@@ -213,7 +219,7 @@
         proto_copy = send_one(proto_all.at[c], proto_all.at[c], partner)
         stud_load.wait()
         put_own(stud_all, unit_along(stud_ref[...], 1)[0])
-        stud_copies = start_gather(stud_all)
+        stud_copies = start_gather(stud_all.at[x], stud_all)
 
     def lanes_of(q):
         start = q * quarter
@@ -225,7 +231,10 @@
         else:
             protos_t = protot_all[half]
             rows_out = pl.ds(pl.multiple_of(half * cols, cols), cols)
-        prod = jnp.dot(protos_t, pair_of(teach_all, block, pair), preferred_element_type=F32)
+        hats = [unit_along(teach_raw[block, q], 1)[0].astype(BF16) for q in pair]
+        prod = lax.dot_general(
+            protos_t, jnp.concatenate(hats, axis=0), NT, preferred_element_type=F32
+        )
         e = jnp.exp2(prod * (LOG2E / TEACHER_TEMP))
         low = e.astype(BF16)
         for i, q in enumerate(pair):
@@ -247,30 +256,32 @@
 
     with scope("s_T_own"):
         acc[...] = jnp.zeros_like(acc)
+        teach_load.wait()
         teacher_part(x, (0, 1), c)
         teacher_part(x, (2, 3), c)
         arrive(protot_copy)
         teacher_part(x, (0, 1), 1 - c)
         teacher_part(x, (2, 3), 1 - c)
-    with scope("s_relay_far"):
-        teach_far = relay_far(teach_all, teach_copies)
+    with scope("s_relay"):
+        teach_near = relay_near(teach_raw, teach_copies)
+        teach_far = relay_far(teach_raw, teach_copies)
     with scope("s_direct"):
-        arrive(teach_copies[1])
+        arrive(teach_copies[2])
+    mine = 2 + lax.rem(z, 2)
     with scope("s_T_early"):
         for k in (1, 3):
-            teacher_part(at_x(k), (y, at_y(1)))
-    with scope("s_direct"):
-        arrive(teach_copies[2])
+            teacher_part(at_x(k), (0, mine))
+    with scope("s_relay_wait"):
+        arrive(teach_copies[3])
+        arrive(teach_near)
     with scope("s_T_late"):
         for k in (1, 3):
-            teacher_part(at_x(k), (at_y(2), at_y(3)))
+            teacher_part(at_x(k), (1, 5 - mine))
     with scope("s_far_wait"):
         arrive(teach_far)
     with scope("s_T_far"):
         teacher_part(at_x(2), (0, 1))
         teacher_part(at_x(2), (2, 3))
-    with scope("s_stud_relay"):
-        stud_far = relay_far(stud_all, stud_copies)
 
     def start_column_scale(step, sums):
         colx[step, c] = sums
@@ -348,9 +359,11 @@
                 r = half_k + q * piece + h * piece // 2
                 send_b[which, q, h, j] = low[r : r + piece // 2]
 
+    B_STEPS = ((2, 1), (3, 0))
+
     def first_groups(which):
-        refs = (far_a, recv_a, far_b, recv_b)
-        return [group(ref.at[which]) for ref in refs]
+        half = far_b.at[which, 0]
+        return [group(ref) for ref in (far_a.at[which], recv_a.at[which], half, recv_b.at[which], half)]
 
     def send_block(which, first, k):
         j = at_x(k)
@@ -362,8 +375,9 @@
         if k == 3:
             send(first[1], send_a.at[which, j, 0], recv_a.at[which, 1, 0], x_dev(j))
         up, down, far = at_y(1), at_y(3), at_y(2)
-        send(first[2], send_b.at[which, far, 0, j], far_b.at[which, 0, j], y_dev(up))
-        send(first[2], send_b.at[which, far, 1, j], far_b.at[which, 1, j], y_dev(down))
+        g = first[2] if k in B_STEPS[0] else first[4]
+        send(g, send_b.at[which, far, 0, j], far_b.at[which, 0, j], y_dev(up))
+        send(g, send_b.at[which, far, 1, j], far_b.at[which, 1, j], y_dev(down))
         send(first[3], send_b.at[which, up, 1, j], recv_b.at[which, 0, 1, j], y_dev(up))
         send(first[3], send_b.at[which, down, 0, j], recv_b.at[which, 1, 0, j], y_dev(down))
 
@@ -374,12 +388,14 @@
             sum_a[which, h] = both.astype(BF16)
             send(first[1], sum_a.at[which, h], recv_a.at[which, h, h], x_dev(at_x(k)))
 
-    def pass_on_b(which, first):
-        arrive(first[2])
+    def pass_on_b(which, first, step):
+        arrive(first[4 if step else 2])
         for h, k in ((0, 1), (1, 3)):
-            both = send_b[which, at_y(k), h].astype(F32) + far_b[which, h].astype(F32)
-            sum_b[which, h] = both.astype(BF16)
-            send(first[3], sum_b.at[which, h], recv_b.at[which, h, h], y_dev(at_y(k)))
+            for i in B_STEPS[step]:
+                j = at_x(i)
+                both = send_b[which, at_y(k), h, j].astype(F32) + far_b[which, h, j].astype(F32)
+                sum_b[which, h, j] = both.astype(BF16)
+                send(first[3], sum_b.at[which, h, j], recv_b.at[which, h, h, j], y_dev(at_y(k)))
 
     def start_second(which, first):
         arrive(first[1])
@@ -434,7 +450,10 @@
         return total
 
     with scope("s_col1"):
-        scale = column_scale(0, first_column_sums())
+        col_copy = start_column_scale(0, first_column_sums())
+        stud_near = relay_near(stud_all, stud_copies)
+        stud_far = relay_far(stud_all, stud_copies)
+        scale = finish_column_scale(0, col_copy)
     with scope("s_row1"):
         xy_copies = start_xy(xy_vec.at[0], row_sums(scale))
     with scope("s_S_own"):
@@ -447,8 +466,9 @@
                         exp_t[j, b * 128 : (b + 1) * 128, a * 128 : (a + 1) * 128]
                     )
     with scope("s_stud_wait"):
-        arrive(stud_copies[1])
         arrive(stud_copies[2])
+        arrive(stud_copies[3])
+        arrive(stud_near)
         student_block(at_x(1))
     with scope("s_xy1"):
         z_copies = start_z(z_vec.at[0], finish(xy_vec.at[0], xy_copies))
@@ -486,7 +506,8 @@
         z_copies = start_z(z_vec.at[1], finish(xy_vec.at[1], xy_copies))
     with scope("s_pass1"):
         pass_on_a(0, first1)
-        pass_on_b(0, first1)
+        pass_on_b(0, first1, 0)
+        pass_on_b(0, first1, 1)
     with scope("s_z2"):
         row_scale = 1.0 / (total_rows * finish(z_vec.at[1], z_copies))
 
@@ -516,11 +537,12 @@
             )
         z_copies = send_z(z_vec.at[2])
     with scope("s_pass2a"):
+        pass_on_b(1, first2, 0)
         pass_on_a(1, first2)
     with scope("s_third1"):
         third1 = start_third(0, second1)
     with scope("s_pass2b"):
-        pass_on_b(1, first2)
+        pass_on_b(1, first2, 1)
 
     with scope("s_second2"):
         second2 = start_second(1, first2)
@@ -675,9 +697,8 @@
         piece = k_dim // 8
         scratch = [
             vmem((own, k_dim), BF16),
-            vmem((own, k_dim), BF16),
             vmem((k_dim, cols), BF16),
-            vmem((NX, 4, k_dim, own // 4), BF16),
+            vmem((NX, 4, own // 4, k_dim), BF16),
             vmem((NX, 4, k_dim, own // 4), BF16),
             vmem((NC, k_dim, cols), BF16),
             vmem((NC, cols, k_dim), BF16),
@@ -730,7 +751,7 @@
                 collective_id=0, has_side_effects=True, vmem_limit_bytes=60 << 20
             ),
             name="prototype_head",
-        )(teacher_emb, student_emb, prototypes)
+        )(teacher_emb.reshape(4, own // 4, k_dim), student_emb, prototypes)
         loss, grad_student, grad_prototypes = pl.pallas_call(
             store_kernel,
             out_shape=tuple(jax.ShapeDtypeStruct(shape, F32) for shape in shapes),

time: 80 us -> 79.4 us (level)
  Pallas kernels: 78.7 us -> 77.4 us
    pallas_call x1, Pallas kernels: 77.5 us -> 76.2 us  [shards(): pl.pallas_call(functools.partial(kernel, float(total_rows), float(total_c...]
where the time goes in v5:
time: 79.4 us; the launch traced here: 78.2 us
  Pallas kernels  77.4 us (97%)
  between operations  0.8 us (1%)
    pallas_call x1, Pallas kernels, shards(): pl.pallas_call(functools.partial(kernel, float(total_rows), float(total_c...  76.2 us

profile of v5, /device:TPU:1, one launch (start us, length us, event | category | flops | bytes accessed | tf_op | source)
XLA Modules:
  0.0 78.2 jit_solution(9395446948536890235)
XLA Ops:
  0.6 76.2 %prototype_head.1 = (f32[1,128]{1,0:T(1,128)S(1)}, f32[512,256]{1,0:T(8,128)S(1)}, f32[256,1024]{1,0:T(8,128)S(1)}) custom-call(bf16[4,128,256]{2,1,0:T(8,128)(2,1)} %bitcast.3, bf16[512,256]{1,0:T(8,128)(2,1)} %stud_hbm.1, bf16[256,1024]{1,0:T(8,128)(2,1)} %proto_hbm.1), custom_call_target="tpu_custom_call" | custom-call | tf_op jit(solution)/shard_map/prototype_head/pallas_call | solution.py:744
  76.8 1.2 %store_results.1 = (f32[1,128]{1,0:T(1,128)}, f32[512,256]{1,0:T(8,128)}, f32[256,1024]{1,0:T(8,128)}) custom-call(f32[1,128]{1,0:T(1,128)S(1)} %get-tuple-element.9.refs_0_, f32[512,256]{1,0:T(8,128)S(1)} %get-tuple-element.10.refs_1_, f32[256,1024]{1,0:T(8,128)S(1)} %get-tuple-element.11.refs_2_), custom_call_target="tpu_custom_call" | custom-call | tf_op jit(solution)/shard_map/store_results/pallas_call | solution.py:755

commit v6 on v5

--- a/solution.py
+++ b/solution.py
@@ -14,7 +14,7 @@
 NORM_EPS = 1e-06
 LOG2E = 1.4426950408889634
 NX, NC, NY, NZ = 4, 2, 4, 8
-GROUPS = 50
+GROUPS = 54
 
 MESH = pl.DeviceIdType.MESH
 scope = jax.named_scope
@@ -58,6 +58,8 @@
     exp_s,
     acc,
     colx,
+    xy_half,
+    z_half,
     xy_vec,
     z_vec,
     xy_loss,
@@ -301,23 +303,35 @@
             parts.append(jnp.sum(t, axis=0, keepdims=True))
         return jnp.concatenate(parts, axis=1)
 
-    def column_sums(row_scale):
-        both = split_rows(row_scale)
+    HALVES = ((0, 1), (2, 3))
+
+    def column_sums(step, z_copies):
         total = None
-        for j in range(NX):
-            part = jnp.dot(
-                both[:, j * own : (j + 1) * own], exp_n[j], preferred_element_type=F32
-            )
-            total = part if total is None else total + part
+        for p, blocks in enumerate(HALVES):
+            row_scale = 1.0 / (total_rows * finish(z_half.at[step, p], z_copies[p]))
+            both = split_rows(row_scale)
+            for i, j in enumerate(blocks):
+                part = jnp.dot(
+                    both[:, i * own : (i + 1) * own], exp_n[j], preferred_element_type=F32
+                )
+                total = part if total is None else total + part
         return total[0:1] + total[1:2]
 
-    def row_sums(col_scale):
+    def start_rows(step, col_scale):
         both = split_rows(col_scale)
-        parts = []
-        for j in range(NX):
-            part = jnp.dot(both, exp_t[j], preferred_element_type=F32)
-            parts.append(part[0:1] + part[1:2])
-        return jnp.concatenate(parts, axis=1)
+        copies = []
+        for p, blocks in enumerate(HALVES):
+            parts = []
+            for j in blocks:
+                part = jnp.dot(both, exp_t[j], preferred_element_type=F32)
+                parts.append(part[0:1] + part[1:2])
+            copies.append(start_xy(xy_half.at[step, p], jnp.concatenate(parts, axis=1)))
+        return copies
+
+    def rows_on_z(step, copies):
+        return [
+            start_z(z_half.at[step, p], finish(xy_half.at[step, p], copies[p])) for p in range(2)
+        ]
 
     xy_me = x * NY + y
 
@@ -455,7 +469,7 @@
         stud_far = relay_far(stud_all, stud_copies)
         scale = finish_column_scale(0, col_copy)
     with scope("s_row1"):
-        xy_copies = start_xy(xy_vec.at[0], row_sums(scale))
+        xy_copies = start_rows(0, scale)
     with scope("s_S_own"):
         student_block(x)
     with scope("s_transpose"):
@@ -471,7 +485,7 @@
         arrive(stud_near)
         student_block(at_x(1))
     with scope("s_xy1"):
-        z_copies = start_z(z_vec.at[0], finish(xy_vec.at[0], xy_copies))
+        z_copies = rows_on_z(0, xy_copies)
     with scope("s_S_near"):
         student_block(at_x(3))
     with scope("s_S_far"):
@@ -487,32 +501,27 @@
             value = jnp.dot(left[...], exp_s[j], preferred_element_type=F32)
             put_block(0, j, value[0:k_dim])
             stud_sums.append(value[k_dim : k_dim + 1])
-        stud_xy = start_xy(xy_vec.at[3], jnp.concatenate(stud_sums, axis=1))
-    with scope("s_z1"):
-        row_scale = 1.0 / (total_rows * finish(z_vec.at[0], z_copies))
-
+        stud_xy = start_xy(xy_vec.at[1], jnp.concatenate(stud_sums, axis=1))
     with scope("s_col2"):
-        sums = column_sums(row_scale)
+        sums = column_sums(0, z_copies)
     with scope("s_colx2"):
         scale = column_scale(1, sums)
     with scope("s_row2"):
-        xy_copies = start_xy(xy_vec.at[1], row_sums(scale))
+        xy_copies = start_rows(1, scale)
         first1 = first_groups(0)
         for k in (2, 1, 3, 0):
             send_block(0, first1, k)
     with scope("s_studxy"):
-        stud_z = start_z(z_vec.at[3], finish(xy_vec.at[3], stud_xy))
+        stud_z = start_z(z_vec.at[1], finish(xy_vec.at[1], stud_xy))
     with scope("s_xy2"):
-        z_copies = start_z(z_vec.at[1], finish(xy_vec.at[1], xy_copies))
+        z_copies = rows_on_z(1, xy_copies)
     with scope("s_pass1"):
         pass_on_a(0, first1)
         pass_on_b(0, first1, 0)
         pass_on_b(0, first1, 1)
-    with scope("s_z2"):
-        row_scale = 1.0 / (total_rows * finish(z_vec.at[1], z_copies))
 
     with scope("s_col3"):
-        sums = column_sums(row_scale)
+        sums = column_sums(1, z_copies)
     with scope("s_colx3"):
         col_copy = start_column_scale(2, sums)
         second1 = start_second(0, first1)
@@ -529,13 +538,13 @@
             value = jnp.dot(left[...], exp_t[j], preferred_element_type=F32)
             put_block(1, j, value[0:k_dim])
             send_block(1, first2, k)
-            z_vec[2, z, :, pl.ds(pl.multiple_of(j * own, own), own)] = (
+            z_vec[0, z, :, pl.ds(pl.multiple_of(j * own, own), own)] = (
                 value[k_dim : k_dim + 1] + value[k_dim + 1 : k_dim + 2]
             )
             cross[j] = jnp.sum(
                 value[0:k_dim] * block_of(stud_all, j).astype(F32), axis=0, keepdims=True
             )
-        z_copies = send_z(z_vec.at[2])
+        z_copies = send_z(z_vec.at[0])
     with scope("s_pass2a"):
         pass_on_b(1, first2, 0)
         pass_on_a(1, first2)
@@ -547,10 +556,10 @@
     with scope("s_second2"):
         second2 = start_second(1, first2)
     with scope("s_z3"):
-        xy_copies = start_xy(xy_vec.at[2], finish(z_vec.at[2], z_copies))
+        xy_copies = start_xy(xy_vec.at[0], finish(z_vec.at[0], z_copies))
 
     with scope("s_dwS"):
-        stud_total = finish(z_vec.at[3], stud_z)
+        stud_total = finish(z_vec.at[1], stud_z)
         stud_factor = (1.0 / STUDENT_TEMP) / stud_total
         for h in range(NC):
             total = None
@@ -569,7 +578,7 @@
     with scope("s_third2"):
         third2 = start_third(1, second2)
     with scope("s_xy3"):
-        row_scale = 1.0 / (total_rows * finish(xy_vec.at[2], xy_copies))
+        row_scale = 1.0 / (total_rows * finish(xy_vec.at[0], xy_copies))
         teach_factor = (total_rows / STUDENT_TEMP) * row_scale
 
     with scope("s_loss"):
@@ -708,8 +717,10 @@
             vmem((NX, both, own), BF16),
             vmem((both, 128), F32),
             vmem((ITERS, NC, 1, both), F32),
-            vmem((ITERS + 1, NX * NY, 1, rows), F32),
-            vmem((ITERS + 1, NZ, 1, rows), F32),
+            vmem((ITERS - 1, 2, NX * NY, 1, rows // 2), F32),
+            vmem((ITERS - 1, 2, NZ, 1, rows // 2), F32),
+            vmem((2, NX * NY, 1, rows), F32),
+            vmem((2, NZ, 1, rows), F32),
             vmem((NX * NY, 1, 128), F32),
             vmem((NZ, 1, 128), F32),
             vmem((2, NX, 2, k_dim // 4, own), BF16),

time: 79.4 us -> 77 us (0.970); the launches traced: 78.2 us -> 76.9 us
  Pallas kernels: 77.4 us -> 76.1 us
    pallas_call x1, Pallas kernels: 76.2 us -> 74.9 us  [shards(): pl.pallas_call(functools.partial(kernel, float(total_rows), float(total_c...]
where the time goes in v6:
time: 77 us; the launch traced here: 76.9 us
  Pallas kernels  76.1 us (99%)
  between operations  0.8 us (1%)
    pallas_call x1, Pallas kernels, shards(): pl.pallas_call(functools.partial(kernel, float(total_rows), float(total_c...  74.9 us

profile of v6, /device:TPU:1, one launch (start us, length us, event | category | flops | bytes accessed | tf_op | source)
XLA Modules:
  0.0 76.9 jit_solution(7190483458651026608)
XLA Ops:
  0.6 74.9 %prototype_head.1 = (f32[1,128]{1,0:T(1,128)S(1)}, f32[512,256]{1,0:T(8,128)S(1)}, f32[256,1024]{1,0:T(8,128)S(1)}) custom-call(bf16[4,128,256]{2,1,0:T(8,128)(2,1)} %bitcast.3, bf16[512,256]{1,0:T(8,128)(2,1)} %stud_hbm.1, bf16[256,1024]{1,0:T(8,128)(2,1)} %proto_hbm.1), custom_call_target="tpu_custom_call" | custom-call | tf_op jit(solution)/shard_map/prototype_head/pallas_call | solution.py:755
  75.6 1.2 %store_results.1 = (f32[1,128]{1,0:T(1,128)}, f32[512,256]{1,0:T(8,128)}, f32[256,1024]{1,0:T(8,128)}) custom-call(f32[1,128]{1,0:T(1,128)S(1)} %get-tuple-element.9.refs_0_, f32[512,256]{1,0:T(8,128)S(1)} %get-tuple-element.10.refs_1_, f32[256,1024]{1,0:T(8,128)S(1)} %get-tuple-element.11.refs_2_), custom_call_target="tpu_custom_call" | custom-call | tf_op jit(solution)/shard_map/store_results/pallas_call | solution.py:766
